TPU v7x, 128 devices: a whole 4x4x4 slice. The times are simulated.
128 devices in a mesh: dp: 2 (over x_lo), ctx: 8 (over z, core), fsdp: 8 (over y, x_hi).
Axes of the slice: x: 4 (x_hi: 2, x_lo: 2; x = x_hi * 2 + x_lo), y: 4, z: 4, core: 2. Of those that a mesh axis runs over, the one named last changes fastest.
Arguments:
- hidden_in: bfloat16 [16, 1024, 1024], P(('dp', 'fsdp'), 'ctx'), may hold values from -6 to 6
- positions: int32 [16, 1024], P(('dp', 'fsdp')), may hold values from 0 to 1023, as said below
- cotangent: bfloat16 [16, 1024, 1024], P(('dp', 'fsdp'), 'ctx'), may hold values from -6 to 6
- attn_gain: float32 [1024], replicated, may hold values from 0.25 to 1.75
- w_query: bfloat16 [1024, 1024], P('fsdp'), may hold values from -0.1875 to 0.1875
- w_key: bfloat16 [1024, 512], P('fsdp'), may hold values from -0.1875 to 0.1875
- w_value: bfloat16 [1024, 512], P('fsdp'), may hold values from -0.1875 to 0.1875
- query_gain: float32 [64], replicated, may hold values from 0.25 to 1.75
- key_gain: float32 [64], replicated, may hold values from 0.25 to 1.75
- w_out: bfloat16 [1024, 1024], P('fsdp'), may hold values from -3 to 3
- ffn_gain: float32 [1024], replicated, may hold values from 0.25 to 1.75
- w_gate: bfloat16 [1024, 4608], P('fsdp'), may hold values from -0.1875 to 0.1875
- w_up: bfloat16 [1024, 4608], P('fsdp'), may hold values from -0.1875 to 0.1875
- w_down: bfloat16 [4608, 1024], P('fsdp'), may hold values from -0.09375 to 0.09375
Outputs:
- block_out: bfloat16 [16, 1024, 1024], P(('dp', 'fsdp'), 'ctx')
- grad_in: bfloat16 [16, 1024, 1024], P(('dp', 'fsdp'), 'ctx')
- grad_attn_gain: float32 [1024], replicated
- grad_w_query: float32 [1024, 1024], P('fsdp')
- grad_w_key: float32 [1024, 512], P('fsdp')
- grad_w_value: float32 [1024, 512], P('fsdp')
- grad_query_gain: float32 [64], replicated
- grad_key_gain: float32 [64], replicated
- grad_w_out: float32 [1024, 1024], P('fsdp')
- grad_ffn_gain: float32 [1024], replicated
- grad_w_gate: float32 [1024, 4608], P('fsdp')
- grad_w_up: float32 [1024, 4608], P('fsdp')
- grad_w_down: float32 [4608, 1024], P('fsdp')
Inputs may be any that keep to these rules, and one draw needn't show every extreme that they name: Each row holds every position once. The 128 entries that start at each multiple of 128 are two blocks of 64 consecutive increasing positions: block b and block 15 - b, in either order, where block b holds positions b * 64 to (b + 1) * 64 - 1.
All inputs are finite; a program needn't handle non-finite values.
Results may differ from a plain program's by a relative error of at most 0.024.
Values may be sent and summed in bfloat16 or wider, within the bound.
No kernel may reach another device: no remote copies, remote signals or barrier semaphores. Data moves between devices by JAX's collectives and lax.ppermute only.
A program may use at most 192 MiB of HBM per device.

v0:
```python
import math

import jax
import jax.numpy as jnp
from jax import lax
from jax.experimental import pallas as pl
from jax.experimental.pallas import tpu as pltpu
from jax.sharding import PartitionSpec as P

NORM_EPSILON = 1e-05
ROPE_BASE = 1000000.0
MASKED_SCORE = -1e30
BF16 = jnp.bfloat16
F32 = jnp.float32
STEPS = (0, -1, 1, 2)


def rms_scale(values):
    return lax.rsqrt(jnp.mean(values * values, axis=-1, keepdims=True) + NORM_EPSILON)


def rope_tables(places, head_size):
    half_width = head_size // 2
    pair_index = jnp.arange(half_width, dtype=F32)
    frequency = ROPE_BASE ** (-2.0 * pair_index / head_size)
    angles = frequency[:, None] * places.astype(F32)[None, :]
    return jnp.cos(angles), jnp.sin(angles)


def call(kernel, out_shapes, scalars, fetched, args, flops, scratch=(), copies=0):
    vmem = pl.BlockSpec(memory_space=pltpu.VMEM)
    operands = (*scalars, *fetched, *args)
    out_bytes = sum(math.prod(o.shape) * o.dtype.itemsize for o in out_shapes)
    in_bytes = sum(math.prod(a.shape) * a.dtype.itemsize for a in operands)
    return pl.pallas_call(
        kernel,
        out_shape=out_shapes,
        in_specs=[pl.BlockSpec(memory_space=pltpu.SMEM)] * len(scalars)
        + [pl.BlockSpec(memory_space=pl.ANY)] * len(fetched)
        + [vmem] * len(args),
        out_specs=[vmem] * len(out_shapes),
        scratch_shapes=list(scratch) + ([pltpu.SemaphoreType.DMA((copies,))] if copies else []),
        compiler_params=pltpu.CompilerParams(vmem_limit_bytes=60 * 2**20),
        cost_estimate=pl.CostEstimate(flops=flops, bytes_accessed=in_bytes + out_bytes, transcendentals=0),
    )(*operands)


def shape(dims, kind):
    return jax.ShapeDtypeStruct(dims, kind)


def head_forward(values, gain, cosine, sine):
    scale = lax.rsqrt(jnp.mean(values * values, axis=0, keepdims=True) + NORM_EPSILON)
    hat = values * scale
    normed = hat * gain
    half = values.shape[0] // 2
    front, back = normed[:half], normed[half:]
    rotated = jnp.concatenate([front * cosine - back * sine, back * cosine + front * sine], axis=0)
    return scale, hat, rotated


def head_backward(grads, hat, scale, gain, cosine, sine):
    half = grads.shape[0] // 2
    front, back = grads[:half], grads[half:]
    d_normed = jnp.concatenate([front * cosine + back * sine, back * cosine - front * sine], axis=0)
    scaled = d_normed * gain
    inner = jnp.mean(hat * scaled, axis=0, keepdims=True)
    return scale * (scaled - hat * inner), jnp.sum(d_normed * hat, axis=1, keepdims=True)


def norm_back(d_normed, normed_hat, scale_values, gain_vector):
    scaled = d_normed * gain_vector
    inner = jnp.mean(normed_hat * scaled, axis=-1, keepdims=True)
    return (scale_values * (scaled - normed_hat * inner), d_normed * normed_hat)


def mm(left, right):
    return jnp.dot(left, right, preferred_element_type=F32)


def mm_t(left, right):
    return lax.dot_general(left, right, (((1,), (1,)), ((), ())), preferred_element_type=F32)


def outer_sum(left, right):
    return lax.dot_general(left, right, (((0,), (0,)), ((), ())), preferred_element_type=F32)


def swap_core(value):
    return lax.ppermute(value, "ctx", [(i, i ^ 1) for i in range(8)])


def move_z(value, step):
    return lax.ppermute(value, "ctx", [(i, (i + 2 * step) % 8) for i in range(8)])


def gather_ctx(block):
    pieces = []
    for step in STEPS:
        mine = block if step == 0 else move_z(block, -step)
        pieces += [mine, swap_core(mine)]
    return pieces


def start_scatter_ctx(mine, received):
    sums = [own + other.astype(F32) for own, other in zip(mine, received)]
    return [sums[0]] + [move_z(sums[slot].astype(BF16), STEPS[slot]) for slot in (3, 1, 2)]


def exchange_ctx(own, other):
    other = swap_core(other)
    out = [None] * 4
    for i, step in enumerate(STEPS):
        both = jnp.stack([own[i], other[i]])
        out[(0, 2, 1, 3)[i]] = move_z(both, step) if step else both
    return out


def stage(*values):
    return lax.optimization_barrier(values)


def transpose_mesh(value, flip=0):
    pairs = [
        ((d * 8 + c) * 8 + f, ((d ^ flip) * 8 + f) * 8 + c) for d in range(2) for c in range(8) for f in range(8)
    ]
    return lax.ppermute(value, ("dp", "ctx", "fsdp"), pairs)


def swap_dp(value):
    return lax.ppermute(value, "dp", [(0, 1), (1, 0)])


def move_y(value, step, flip=0):
    pairs = [(y * 2 + x, (y + step) % 4 * 2 + (x ^ flip)) for y in range(4) for x in range(2)]
    return lax.ppermute(value, "fsdp", pairs)


def pair_x(block):
    other = move_y(block, 0, 1)
    first = lax.axis_index("fsdp") % 2 == 0
    return jnp.concatenate([jnp.where(first, block, other), jnp.where(first, other, block)], axis=0)


def spread_y(pair):
    return [pair] + [move_y(pair, step) for step in (1, 3, 2)]


def fetch(pairs, sems, first=0):
    copies = [pltpu.make_async_copy(src, dst, sems.at[first + i]) for i, (src, dst) in enumerate(pairs)]
    for copy in copies:
        copy.start()
    return copies


def rows_of(pieces, ref):
    count = pieces[0].shape[0]
    return [(piece, ref.at[pl.ds(i * count, count)]) for i, piece in enumerate(pieces)]


def joined_y(place, pairs, ref):
    rows = pairs[0].shape[0]
    owners = [(place[0] + 4 - step) % 4 for step in (0, 1, 3, 2)]
    return [(pair, ref.at[pl.ds(pl.multiple_of(y * rows, rows), rows)]) for y, pair in zip(owners, pairs)]


def wait(copies):
    for copy in copies:
        copy.wait()


def all_to_all(blocks, axis):
    return lax.all_to_all(blocks, axis, split_axis=0, concat_axis=0, tiled=True)


def own_columns(weight, width, index):
    return lax.dynamic_slice_in_dim(weight, index * width, width, 1)


def attend_forward(*refs):
    pieces, w_whole, refs = refs[:8], refs[8], refs[9:]
    cos_ref, sin_ref, column_ref, row_ref, q_gain, k_gain = refs[:6]
    qkv_ref, lse_ref, own_ref, other_ref, x_ref, w_qkv, sems = refs[6:]
    w_copies = fetch([(w_whole, w_qkv)], sems, 8)
    x_copies = fetch(rows_of(pieces, x_ref), sems)
    wait(w_copies)
    length = qkv_ref.shape[1]
    count = length // 8
    head = q_gain.shape[0]
    for pair in range(4):
        wait(x_copies[2 * pair : 2 * pair + 2])
        lanes = slice(pair * 2 * count, (pair + 1) * 2 * count)
        qkv_ref[:, lanes] = jnp.transpose(mm(x_ref[lanes], w_qkv[...]))
    cosine, sine = cos_ref[...], sin_ref[...]
    queries = [
        head_forward(qkv_ref[h * head : (h + 1) * head], q_gain[...], cosine, sine)[2].astype(BF16) * BF16(head**-0.5)
        for h in range(2)
    ]
    key = jnp.transpose(head_forward(qkv_ref[2 * head : 3 * head], k_gain[...], cosine, sine)[2]).astype(BF16)
    value = qkv_ref[3 * head :].astype(BF16)
    width = column_ref.shape[1]
    for tile in range(length // width):
        lanes = slice(tile * width, (tile + 1) * width)
        allowed = column_ref[...] <= row_ref[:, lanes]
        outs = []
        for h in range(2):
            scores = jnp.where(allowed, mm(key, queries[h][:, lanes]), MASKED_SCORE)
            top = jnp.max(scores, axis=0, keepdims=True)
            weights = jnp.exp(scores - top)
            total = jnp.sum(weights, axis=0, keepdims=True)
            lse_ref[h : h + 1, lanes] = top + jnp.log(total)
            outs.append(mm(value, (weights * (1.0 / total)).astype(BF16)))
        mixed = jnp.transpose(jnp.concatenate(outs, axis=0)).astype(BF16)
        own_ref[tile] = mixed[:count]
        other_ref[tile] = mixed[count:]


def out_project(place, order, *refs):
    out_pairs, blocks, (tokens, gain, resid_ref, normed_ref, w_out, mixed_ref, sems) = refs[:4], refs[4:8], refs[8:]
    copies = fetch(joined_y(place, out_pairs, w_out), sems)
    count = blocks[0].shape[2]
    for i in range(8):
        lanes = pl.ds(pl.multiple_of(order[i] * count, count), count)
        mixed_ref[:, lanes] = blocks[i // 2][i % 2]
    wait(copies)
    resid = tokens[...].astype(F32) + mm(mixed_ref[...], w_out[...])
    resid_ref[...] = resid
    normed_ref[...] = (resid * rms_scale(resid) * gain[...]).astype(BF16)


def resid_backward(place, order, *refs):
    out_pairs, refs = refs[:4], refs[4:]
    total, move_a, move_b, move_c, resid_ref, cot_ref, gain_ref = refs[:7]
    d_resid_ref, d_attn_ref, gain_part_ref, own_ref, other_ref, w_out, d_mixed_ref, sems = refs[7:]
    copies = fetch(joined_y(place, out_pairs, w_out), sems)
    d_second = total[...] + move_a[...].astype(F32) + move_b[...].astype(F32) + move_c[...].astype(F32)
    resid = resid_ref[...]
    scale = rms_scale(resid)
    d_from, gain_part = norm_back(d_second, resid * scale, scale, gain_ref[...])
    gain_part_ref[...] = jnp.sum(gain_part, axis=0, keepdims=True)
    d_resid = cot_ref[...].astype(F32) + d_from
    d_resid_ref[...] = d_resid
    d_attn = d_resid.astype(BF16)
    d_attn_ref[...] = d_attn
    wait(copies)
    d_mixed_ref[...] = mm_t(d_attn, w_out[...]).astype(BF16)
    count = own_ref.shape[2]
    for i in range(8):
        lanes = pl.ds(pl.multiple_of(order[i] * count, count), count)
        (own_ref, other_ref)[i % 2][i // 2] = d_mixed_ref[:, lanes]


def attend_backward(*refs):
    order, w_whole, d_blocks, refs = refs[0], refs[1], refs[2:6], refs[6:]
    cos_ref, sin_ref, column_ref, row_ref, q_gain, k_gain, qkv_ref, lse_ref = refs[:8]
    q_gain_ref, k_gain_ref, d_low_ref, d_first_ref, d_qkv_ref, w_qkv, sems = refs[8:]
    copies = fetch([(w_whole, w_qkv)], sems)
    length = qkv_ref.shape[1]
    head = q_gain.shape[0]
    count = length // 8
    cosine, sine = cos_ref[...], sin_ref[...]
    scales, hats, queries = [], [], []
    for h in range(2):
        scale, hat, rotated = head_forward(qkv_ref[h * head : (h + 1) * head], q_gain[...], cosine, sine)
        scales.append(scale)
        hats.append(hat)
        queries.append(rotated.astype(BF16) * BF16(head**-0.5))
    k_scale, k_hat, rotated = head_forward(qkv_ref[2 * head : 3 * head], k_gain[...], cosine, sine)
    key_rows = rotated.astype(BF16)
    key = jnp.transpose(rotated).astype(BF16)
    value = jnp.transpose(qkv_ref[3 * head :]).astype(BF16)
    width = column_ref.shape[1]
    d_key = jnp.zeros((length, head), F32)
    d_value = jnp.zeros((length, head), F32)
    for tile in range(length // width):
        lanes = slice(tile * width, (tile + 1) * width)
        allowed = column_ref[...] <= row_ref[:, lanes]
        d_mixed = jnp.concatenate([d_blocks[tile][0], d_blocks[tile][1]], axis=0)
        d_mixed = jnp.transpose(d_mixed.astype(F32)).astype(BF16)
        for h in range(2):
            rows = slice(h * head, (h + 1) * head)
            query = queries[h][:, lanes]
            probs = jnp.where(allowed, jnp.exp(mm(key, query) - lse_ref[h : h + 1, lanes]), 0.0)
            d_probs = mm(value, d_mixed[rows])
            inner = jnp.sum(probs * d_probs, axis=0, keepdims=True)
            d_scores = (probs * (d_probs - inner)).astype(BF16)
            d_value += mm_t(probs.astype(BF16), d_mixed[rows])
            d_key += mm_t(d_scores, query)
            d_qkv_ref[rows, lanes] = mm(key_rows, d_scores) * head**-0.5
    for h in range(2):
        rows = slice(h * head, (h + 1) * head)
        d_query, gain_part = head_backward(d_qkv_ref[rows], hats[h], scales[h], q_gain[...], cosine, sine)
        d_qkv_ref[rows] = d_query
        if h == 0:
            q_gain_ref[...] = gain_part
        else:
            q_gain_ref[...] += gain_part
    d_keys, gain_part = head_backward(jnp.transpose(d_key), k_hat, k_scale, k_gain[...], cosine, sine)
    k_gain_ref[...] = gain_part
    d_qkv_ref[2 * head : 3 * head] = d_keys
    d_qkv_ref[3 * head :] = jnp.transpose(d_value)
    wait(copies)
    for tile in range(4):
        lanes = slice(tile * 2 * count, (tile + 1) * 2 * count)
        d_qkv = jnp.transpose(d_qkv_ref[:, lanes]).astype(BF16)
        d_low_ref[lanes] = d_qkv
        d_first = mm_t(d_qkv, w_qkv[...])
        d_first_ref[order[2 * tile]] = d_first[:count].astype(BF16)
        d_first_ref[order[2 * tile + 1]] = d_first[count:].astype(BF16)


def attend_weights(*refs):
    pieces, d_pieces, own, other, w_whole = refs[:8], refs[8:16], *refs[16:19]
    d_low, attn_gain, ffn_part, q_part, k_part = refs[19:24]
    out_ref, x_ref, d_ref, mixed_ref, d_low_ref, w_qkv, sems = refs[24:]
    count = pieces[0].shape[0]
    width = d_low_ref.shape[1]
    mixed = []
    for i in range(4):
        mixed += [(own.at[i], mixed_ref.at[pl.ds(2 * i * count, count)])]
        mixed += [(other.at[i], mixed_ref.at[pl.ds((2 * i + 1) * count, count)])]
    copies = fetch([(d_low, d_low_ref), *rows_of(pieces, x_ref), (w_whole, w_qkv)], sems)
    more = fetch([*mixed, *rows_of(d_pieces, d_ref)], sems, len(copies))
    wait(copies)
    grad_qkv = outer_sum(d_low_ref[...], x_ref[...])
    attn_part = jnp.sum(grad_qkv * jnp.transpose(w_qkv[...].astype(F32)), axis=0, keepdims=True) / attn_gain[...]
    grad_qkv = jnp.transpose(grad_qkv).astype(BF16)
    wait(more)
    grad_out = jnp.transpose(outer_sum(mixed_ref[...], d_ref[...])).astype(BF16)
    lines = [part[:, i * 128 : (i + 1) * 128] for part in (attn_part, ffn_part[...]) for i in range(8)]
    lines.append(jnp.concatenate([jnp.transpose(q_part[...]), jnp.transpose(k_part[...])], axis=1))
    gains = jnp.concatenate(lines + [jnp.zeros((7, 128), F32)], axis=0)
    high = gains.astype(BF16)
    low = (gains - high.astype(F32)).astype(BF16)
    gains = jnp.concatenate([high, low, jnp.zeros((count - 48, 128), BF16)], axis=0)
    for i in range(8):
        rows = slice(i * count, (i + 1) * count)
        out_ref[i, :, :width] = grad_qkv[rows]
        out_ref[i, :, width : width + 128] = gains
        out_ref[i, :, width + 128 :] = grad_out[rows]


def ffn(*refs):
    order, seconds, cots, weights = refs[0], refs[1:9], refs[9], refs[10]
    hidden_ref, d_ffn_ref, block_ref, d_send = refs[11:15]
    d_mine, (x_ref, cot_ref, w_ref, sems) = refs[15:19], refs[19:]
    copies = fetch([(weights, w_ref)], sems)
    loads = rows_of(seconds, x_ref) + rows_of([cots.at[order[i]] for i in range(8)], cot_ref)
    loads = fetch([loads[8 * j + 2 * g + i] for g in (3, 1, 2, 0) for j in (0, 1) for i in (0, 1)], sems, 1)
    wait(copies)
    width = hidden_ref.shape[1]
    count = seconds[0].shape[0]
    for group in (3, 1, 2, 0):
        rows = slice(2 * group * count, 2 * (group + 1) * count)
        wait(loads[:4])
        loads = loads[4:]
        x, cot = x_ref[rows], cot_ref[rows]
        both = mm(x, w_ref[:, : 2 * width])
        gate, up = both[:, :width], both[:, width:]
        sigmoid = 1.0 / (1.0 + jnp.exp(-gate))
        act = gate * sigmoid
        hidden = (act * up).astype(BF16)
        hidden_ref[rows] = hidden
        d_hidden = mm(cot, w_ref[:, 2 * width :])
        d_gate = d_hidden * up * sigmoid * (1.0 + gate * (1.0 - sigmoid))
        d_ffn = jnp.concatenate([d_gate, d_hidden * act], axis=1).astype(BF16)
        d_ffn_ref[rows] = d_ffn
        d_second = mm_t(d_ffn, w_ref[:, : 2 * width])
        d_mine[group][...] = d_second[:count]
        d_send[group] = d_second[count:].astype(BF16)
        out = mm_t(hidden, w_ref[:, 2 * width :])
        block_ref[order[2 * group]] = out[:count].astype(BF16)
        block_ref[order[2 * group + 1]] = out[count:].astype(BF16)


def ffn_weights(*refs):
    order, seconds, cots, hidden, d_ffn = refs[0], refs[1:9], *refs[9:12]
    out_ref, x_ref, cot_ref, hidden_ref, d_ffn_ref, sems = refs[12:]
    count = seconds[0].shape[0]
    copies = fetch([(d_ffn, d_ffn_ref), *rows_of(seconds, x_ref)], sems)
    more = fetch([(hidden, hidden_ref), *rows_of([cots.at[order[i]] for i in range(8)], cot_ref)], sems, 9)
    for left_ref, right_ref, columns in ((x_ref, d_ffn_ref, 0), (cot_ref, hidden_ref, d_ffn_ref.shape[1])):
        wait(more if columns else copies)
        width = right_ref.shape[1]
        for pair in range(4):
            both = outer_sum(left_ref[:, 2 * pair * count : 2 * (pair + 1) * count], right_ref[...]).astype(BF16)
            out_ref[2 * pair, :, columns : columns + width] = both[:count]
            out_ref[2 * pair + 1, :, columns : columns + width] = both[count:]
    used = d_ffn_ref.shape[1] + hidden_ref.shape[1]
    out_ref[:, :, used:] = jnp.zeros((8, count, out_ref.shape[2] - used), BF16)


def sum_ffn(parts, gate_up_ref, down_ref):
    width = gate_up_ref.shape[1]
    total = sum(parts[i].astype(F32) for i in range(8)).astype(BF16)
    gate_up_ref[...] = total[:, :width]
    down_ref[...] = total[:, width : width + down_ref.shape[1]]


def sum_attn(parts, first_ref, out_ref):
    count = out_ref.shape[0]
    width = first_ref.shape[1] - 128
    total = sum(parts[i].astype(F32) for i in range(8))
    first_ref[:, :width] = total[:, :width].astype(BF16)
    pack_gains(first_ref, width, total[:24, width : width + 128] + total[24:48, width : width + 128])
    out_ref[...] = total[:, width + 128 :].astype(BF16)


def pack_gains(ref, width, gains):
    high = gains.astype(BF16)
    low = (gains - high.astype(F32)).astype(BF16)
    rest = jnp.zeros((ref.shape[0] - 48, 128), BF16)
    ref[:, width : width + 128] = jnp.concatenate([high, low, rest], axis=0)


def join_ffn(own, other, down, down_other, out_ref):
    width = own.shape[1]
    out_ref[:, :width] = (own[...].astype(F32) + other[...].astype(F32)).astype(BF16)
    out_ref[:, width:] = (down[...].astype(F32) + down_other[...].astype(F32)).astype(BF16)


def join_attn(own, other, out, out_other, out_ref):
    width = own.shape[1] - 128
    total = own[...].astype(F32) + other[...].astype(F32)
    out_ref[:, :width] = total[:, :width].astype(BF16)
    pack_gains(out_ref, width, total[:24, width:] + total[24:48, width:])
    out_ref[:, width + 128 :] = (out[...].astype(F32) + out_other[...].astype(F32)).astype(BF16)


def assemble_ffn(*refs):
    order, pieces, (gate_ref, up_ref, down_ref, held, sems) = refs[0], refs[1:9], refs[9:]
    width = down_ref.shape[0]
    count = pieces[0].shape[0]
    wait(fetch([(pieces[i], held.at[order[i]]) for i in range(8)], sems))
    for owner in range(8):
        columns = slice(owner * width, (owner + 1) * width)
        gate_ref[:, columns] = held[owner, :, :width].astype(F32)
        up_ref[:, columns] = held[owner, :, width : 2 * width].astype(F32)
        down = held[owner, :, 2 * width :].astype(F32)
        down_ref[:, owner * count : (owner + 1) * count] = jnp.transpose(down)


def assemble_attn(*refs):
    order, pieces, (query_ref, key_ref, value_ref, out_ref, gains_ref, held, sems) = refs[0], refs[1:9], refs[9:]
    count = pieces[0].shape[0]
    half = count // 2
    wait(fetch([(pieces[i], held.at[order[i]]) for i in range(8)], sems))
    gains = jnp.zeros(gains_ref.shape, F32)
    for owner in range(8):
        columns = slice(owner * count, (owner + 1) * count)
        narrow = slice(owner * half, (owner + 1) * half)
        part = held[owner].astype(F32)
        query_ref[:, columns] = part[:, :count]
        key_ref[:, narrow] = part[:, count : count + half]
        value_ref[:, narrow] = part[:, count + half : 2 * count]
        out_ref[:, columns] = jnp.transpose(part[:, 3 * count :])
        gains += part[:24, 2 * count : 3 * count] + part[24:48, 2 * count : 3 * count]
    gains_ref[...] = gains


def body(
    hidden_in,
    positions,
    cotangent,
    attn_gain,
    w_query,
    w_key,
    w_value,
    query_gain,
    key_gain,
    w_out,
    ffn_gain,
    w_gate,
    w_up,
    w_down,
):
    ctx = lax.axis_index("ctx")
    tokens = hidden_in[0].astype(F32)
    count, width = tokens.shape
    head_size = query_gain.shape[0]
    q_width = w_query.shape[1] // 8
    k_width = w_key.shape[1] // 8
    ff_width = w_gate.shape[1] // 8

    z_index, core = ctx // 2, ctx % 2
    owners = jnp.stack(
        [((z_index + step) % 4) * 2 + (core ^ flip) for step in STEPS for flip in (0, 1)]
    )
    places = positions[0].reshape(8, count)[owners].reshape(8 * count)
    length = 8 * count
    cosine_table, sine_table = rope_tables(places, head_size)
    column = jnp.broadcast_to(places[:, None], (length, 2 * count))
    row = places[None]
    gains = (query_gain[:, None], key_gain[:, None])
    tables = (cosine_table, sine_table, column, row)
    block = shape((count, q_width), BF16)
    low_rows, rows = shape((count, width), BF16), shape((count, width), F32)
    qkv_width = q_width + 2 * k_width

    place = jnp.stack([lax.axis_index("fsdp") // 2, lax.axis_index("fsdp") % 2])
    wide, head_rows = pltpu.VMEM((length, width), BF16), pltpu.VMEM((length, qkv_width), BF16)

    first_scale = rms_scale(tokens)
    first_hat = tokens * first_scale
    first_normed = (first_hat * attn_gain).astype(BF16)
    first_pieces = gather_ctx(first_normed)
    qkv_block = jnp.concatenate(
        [own_columns(w_query, q_width, ctx), own_columns(w_key, k_width, ctx), own_columns(w_value, k_width, ctx)],
        axis=1,
    )
    w_qkv = all_to_all(jnp.broadcast_to(qkv_block[None], (8, *qkv_block.shape)), "fsdp").reshape(width, qkv_width)
    out_pair = pair_x(w_out)
    cot = cotangent[0]
    cot_copies = jnp.broadcast_to(cot[None], (8, count, width))
    down_chunk = transpose_mesh(jnp.transpose(own_columns(w_down, width // 8, ctx)))
    ffn_block = jnp.concatenate(
        [own_columns(w_gate, ff_width, ctx), own_columns(w_up, ff_width, ctx), down_chunk], axis=1
    )
    ffn_block, w_qkv = stage(ffn_block, w_qkv)
    ffn_rows = lax.all_gather(ffn_block, "fsdp", axis=0, tiled=True)
    first_pieces, w_qkv, tables, out_pair, cot_copies = stage(first_pieces, w_qkv, tables, out_pair, cot_copies)

    cots = all_to_all(cot_copies, "ctx")
    out_pairs = spread_y(out_pair)
    qkv, lse, own, other = call(
        attend_forward,
        [shape((qkv_width, length), F32), shape((8, length), F32)] + [shape((4, count, q_width), BF16)] * 2,
        (),
        (*first_pieces, w_qkv),
        (*tables, *gains),
        4 * 10**9,
        [wide, pltpu.VMEM((width, qkv_width), BF16)],
        9,
    )

    mixed_blocks = exchange_ctx(own, other)
    mixed_blocks, out_pairs = stage(mixed_blocks, out_pairs)
    square = pltpu.VMEM((width, width), BF16)
    residual, second_normed = call(
        out_project,
        [rows, low_rows],
        (place, owners),
        out_pairs,
        (*mixed_blocks, hidden_in[0], ffn_gain[None]),
        3 * 10**8,
        [square, pltpu.VMEM((count, width), BF16)],
        4,
    )

    second_pieces = gather_ctx(second_normed)
    hidden_shape, d_ffn_shape = shape((length, ff_width), BF16), shape((length, 2 * ff_width), BF16)
    hidden, d_ffn, block_parts, d_send, *d_mine = call(
        ffn,
        [hidden_shape, d_ffn_shape, shape((8, count, width), BF16), shape((4, count, width), BF16)] + [rows] * 4,
        (owners,),
        (*second_pieces, cots, ffn_rows),
        (),
        8 * 10**9,
        [wide, wide, pltpu.VMEM((width, 3 * ff_width), BF16)],
        17,
    )

    d_moves = start_scatter_ctx(d_mine, swap_core(d_send))
    padded = -(-3 * ff_width // 128) * 128
    (ffn_partial,) = call(
        ffn_weights,
        [shape((8, count, padded), BF16)],
        (owners,),
        (*second_pieces, cots, hidden, d_ffn),
        (),
        4 * 10**9,
        [wide, wide, pltpu.VMEM((length, ff_width), BF16), pltpu.VMEM((length, 2 * ff_width), BF16)],
        18,
    )
    ffn_sums = all_to_all(ffn_partial, "fsdp")
    d_moves, _ = stage(d_moves, ffn_partial)
    block_sum = lax.psum_scatter(block_parts, "ctx", scatter_dimension=0, tiled=False)
    block_out = (residual + block_sum.astype(F32)).astype(BF16)
    d_resid, d_attn, ffn_gain_part, *d_blocks = call(
        resid_backward,
        [rows, low_rows, shape((1, width), F32)] + [shape((4, count, q_width), BF16)] * 2,
        (place, owners),
        out_pairs,
        (*d_moves, residual, cot, ffn_gain[None]),
        3 * 10**8,
        [square, pltpu.VMEM((count, width), BF16)],
        4,
    )

    d_blocks = exchange_ctx(*d_blocks)
    d_blocks, d_attn = stage(d_blocks, d_attn)

    d_pieces = gather_ctx(d_attn)
    q_gain_part, k_gain_part, d_qkv, d_first_parts = call(
        attend_backward,
        [
            shape((head_size, 1), F32),
            shape((head_size, 1), F32),
            shape((length, qkv_width), BF16),
            shape((8, count, width), BF16),
        ],
        (owners,),
        (w_qkv,),
        (*d_blocks, *tables, *gains, qkv, lse),
        8 * 10**9,
        [pltpu.VMEM((qkv_width, length), F32), pltpu.VMEM((width, qkv_width), BF16)],
        1,
    )
    half, down = call(
        sum_ffn, [shape((count, 2 * ff_width), BF16), shape((count, ff_width), BF16)], (), (), (ffn_sums,), 10**6
    )
    d_qkv, d_pieces, half, down = stage(d_qkv, d_pieces, half, down)
    ffn_steps = (half, swap_dp(half), transpose_mesh(down), transpose_mesh(down, 1))
    d_first = lax.psum_scatter(d_first_parts, "ctx", scatter_dimension=0, tiled=False).astype(F32)
    (attn_partial,) = call(
        attend_weights,
        [shape((8, count, qkv_width + 128 + q_width), BF16)],
        (),
        (*first_pieces, *d_pieces, own, other, w_qkv, d_qkv),
        (attn_gain[None], ffn_gain_part, q_gain_part, k_gain_part),
        10**9,
        [wide, wide, pltpu.VMEM((length, q_width), BF16), head_rows, pltpu.VMEM((width, qkv_width), BF16)],
        26,
    )
    attn_partial, ffn_steps = stage(attn_partial, ffn_steps)

    attn_sums = all_to_all(attn_partial, "fsdp")
    (joined,) = call(
        join_ffn,
        [shape((count, 3 * ff_width), BF16)],
        (),
        (),
        ffn_steps,
        10**6,
    )
    ffn_parts = gather_ctx(joined)
    half, out = call(
        sum_attn, [shape((count, qkv_width + 128), BF16), shape((count, q_width), BF16)], (), (), (attn_sums,), 10**6
    )
    (joined,) = call(
        join_attn,
        [shape((count, qkv_width + 128 + q_width), BF16)],
        (),
        (),
        (half, swap_dp(half), transpose_mesh(out), transpose_mesh(out, 1)),
        10**6,
    )
    attn_parts = gather_ctx(joined)
    d_from_first, _ = norm_back(d_first, first_hat, first_scale, attn_gain)
    grad_in = (d_resid + d_from_first).astype(BF16)
    grad_gate, grad_up, grad_down = call(
        assemble_ffn,
        [shape((count, 8 * ff_width), F32)] * 2 + [shape((ff_width, width), F32)],
        (owners,),
        ffn_parts,
        (),
        10**6,
        [pltpu.VMEM((8, count, 3 * ff_width), BF16)],
        8,
    )
    grad_query, grad_key, grad_value, grad_out, totals = call(
        assemble_attn,
        [shape((count, width), F32)] + [shape((count, 8 * k_width), F32)] * 2 + [shape((q_width, width), F32), shape((24, 128), F32)],
        (owners,),
        attn_parts,
        (),
        10**6,
        [pltpu.VMEM((8, count, qkv_width + 128 + q_width), BF16)],
        8,
    )
    totals = totals.reshape(-1)
    grad_attn_gain = totals[:width]
    grad_ffn_gain = totals[width : 2 * width]
    grad_query_gain = totals[2 * width : 2 * width + head_size]
    grad_key_gain = totals[2 * width + head_size : 2 * width + 2 * head_size]
    return (
        block_out[None],
        grad_in[None],
        grad_attn_gain,
        grad_query,
        grad_key,
        grad_value,
        grad_query_gain,
        grad_key_gain,
        grad_out,
        grad_ffn_gain,
        grad_gate,
        grad_up,
        grad_down,
    )


def solution(mesh):
    in_specs = (
        P(("dp", "fsdp"), "ctx", None),
        P(("dp", "fsdp"), None),
        P(("dp", "fsdp"), "ctx", None),
        P(),
        P("fsdp", None),
        P("fsdp", None),
        P("fsdp", None),
        P(),
        P(),
        P("fsdp", None),
        P(),
        P("fsdp", None),
        P("fsdp", None),
        P("fsdp", None),
    )
    out_specs = (
        P(("dp", "fsdp"), "ctx", None),
        P(("dp", "fsdp"), "ctx", None),
        P(),
        P("fsdp", None),
        P("fsdp", None),
        P("fsdp", None),
        P(),
        P(),
        P("fsdp", None),
        P(),
        P("fsdp", None),
        P("fsdp", None),
        P("fsdp", None),
    )
    return jax.shard_map(body, mesh=mesh, in_specs=in_specs, out_specs=out_specs, check_vma=False)
```

profile of v0, /device:TPU:31, one launch (start us, length us, event | category | flops | bytes accessed | tf_op | source)
XLA Modules:
  0.0 328.2 jit_solution(8735067585858316334)
XLA Ops:
  9.9 6.7 %all-to-all-start = ((bf16[8,128,256]{2,1,0:T(8,128)(2,1)}), bf16[8,128,256]{2,1,0:T(8,128)(2,1)S(1)}, u32[]{:S(2)}, u32[]{:S(2)}) async-start(bf16[8,128,256]{2,1,0:T(8,128)(2,1)} %broadcast_in_dim.20), calls=%async_computation | async-start | bytes 1048576 | tf_op jit(solution)/shard_map/all_to_all | solution.py:173
  16.8 5.7 %collective-permute-start.7 = (bf16[128,576]{1,0:T(8,128)(2,1)S(1)}, bf16[128,576]{1,0:T(8,128)(2,1)S(1)}, u32[]{:S(2)}, u32[]{:S(2)}) collective-permute-start(bf16[128,576]{1,0:T(8,128)(2,1)S(1)} %bitcast.79), channel_id=1, source_target_pairs={{0,0},{1,8},{2,16},{3,24},{4,32},{5,40},{6,48},{7,56},{8,1},{9,9},... | collective-permute-start | bytes 442376 | tf_op jit(solution)/shard_map/ppermute | solution.py:127
  23.7 10.2 %collective-permute-done.7 = bf16[128,576]{1,0:T(8,128)(2,1)S(1)} collective-permute-done((bf16[128,576]{1,0:T(8,128)(2,1)S(1)}, bf16[128,576]{1,0:T(8,128)(2,1)S(1)}, u32[]{:S(2)}, u32[]{:S(2)}) %collective-permute-start.7) | collective-permute-done | bytes 147488 | tf_op jit(solution)/shard_map/ppermute | solution.py:127
  35.6 2.7 collective-permute-start.3
  59.6 6.7 %all-to-all-start.1 = ((bf16[8,128,1024]{2,1,0:T(8,128)(2,1)}), bf16[8,128,1024]{2,1,0:T(8,128)(2,1)S(1)}, u32[]{:S(2)}, u32[]{:S(2)}) async-start(bf16[8,128,1024]{2,1,0:T(8,128)(2,1)} %broadcast_in_dim.23), calls=%async_computation.1 | async-start | bytes 4194304 | tf_op jit(solution)/shard_map/all_to_all | solution.py:173
  66.5 11.9 %shard_map.237 = (f32[256,1024]{1,0:T(8,128)}, f32[8,1024]{1,0:T(8,128)}, bf16[4,128,128]{2,1,0:T(8,128)(2,1)}, bf16[4,128,128]{2,1,0:T(8,128)(2,1)}) custom-call(bf16[128,1024]{1,0:T(8,128)(2,1)} %copy-done.10, bf16[128,1024]{1,0:T(8,128)(2,1)} %copy-done.24, bf16[128,1024]{1,0:T(8,128)(2,1)} %copy-done.23, bf16[128,1024]{1,0:T(8,128)(2,1)} %copy-done.27, ...), custom_call_target="tpu_custom_call" | custom-call | flops 4000000000 | bytes 5280256 | tf_op jit(solution)/shard_map/pallas_call | solution.py:35
  82.9 11.1 %collective-permute-done.10.refs_5_ = bf16[2,128,128]{2,1,0:T(8,128)(2,1)S(1)} collective-permute-done((bf16[2,128,128]{2,1,0:T(8,128)(2,1)S(1)}, bf16[2,128,128]{2,1,0:T(8,128)(2,1)S(1)}, u32[]{:S(2)}, u32[]{:S(2)}) %collective-permute-start.10) | collective-permute-done | bytes 65568 | tf_op jit(solution)/shard_map/ppermute | solution.py:94
  95.1 3.9 %collective-permute-done.12.refs_7_ = bf16[2,128,128]{2,1,0:T(8,128)(2,1)S(1)} collective-permute-done((bf16[2,128,128]{2,1,0:T(8,128)(2,1)S(1)}, bf16[2,128,128]{2,1,0:T(8,128)(2,1)S(1)}, u32[]{:S(2)}, u32[]{:S(2)}) %collective-permute-start.12) | collective-permute-done | bytes 65568 | tf_op jit(solution)/shard_map/ppermute | solution.py:94
  99.8 4.0 %shard_map.238 = (f32[128,1024]{1,0:T(8,128)}, bf16[128,1024]{1,0:T(8,128)(2,1)}) custom-call(s32[2]{0:T(128)} %pad_add_fusion.place, s32[8]{0:T(128)} %stack.89.order.refs_0_, bf16[256,1024]{1,0:T(8,128)(2,1)} %copy-done.4, bf16[256,1024]{1,0:T(8,128)(2,1)} %collective-permute-done.13.refs_1_, bf16[256,1024]{1,0:T(8,128)(2,1)} %collective-permute-done.14.refs_2_, ...), custom_call_target="tpu_custom_call" | custom-call | flops 300000000 | bytes 3412008 | tf_op jit(solution)/shard_map/pallas_call | solution.py:35
  108.1 4.1 %collective-permute-done.21.refs_7_ = bf16[128,1024]{1,0:T(8,128)(2,1)S(1)} collective-permute-done((bf16[128,1024]{1,0:T(8,128)(2,1)}, bf16[128,1024]{1,0:T(8,128)(2,1)S(1)}, u32[]{:S(2)}, u32[]{:S(2)}) %collective-permute-start.21) | collective-permute-done | bytes 262176 | tf_op jit(solution)/shard_map/ppermute | solution.py:94
  112.2 4.2 %collective-permute-start.22 = (bf16[128,1024]{1,0:T(8,128)(2,1)S(1)}, bf16[128,1024]{1,0:T(8,128)(2,1)S(1)}, u32[]{:S(2)}, u32[]{:S(2)}) collective-permute-start(bf16[128,1024]{1,0:T(8,128)(2,1)S(1)} %collective-permute-done.21.refs_7_), channel_id=1, source_target_pairs={{0,8},{8,0},{16,24},{24,16},{32,40},{40,32},{48,56},{56,48},{1,9},... | collective-permute-start | bytes 786440 | tf_op jit(solution)/shard_map/ppermute | solution.py:90
  123.0 15.3 %shard_map.239 = (bf16[1024,576]{1,0:T(8,128)(2,1)}, bf16[1024,1152]{1,0:T(8,128)(2,1)}, bf16[8,128,1024]{2,1,0:T(8,128)(2,1)}, bf16[4,128,1024]{2,1,0:T(8,128)(...) custom-call(s32[8]{0:T(128)} %stack.89.order.refs_0_, ...), custom_call_target="tpu_custom_call" | custom-call | flops 8000000000 | bytes 16515104 | tf_op jit(solution)/shard_map/pallas_call | solution.py:35
  142.6 2.7 collective-permute-start.25
  145.2 9.9 %shard_map.240 = bf16[8,128,1792]{2,1,0:T(8,128)(2,1)} custom-call(s32[8]{0:T(128)} %stack.89.order.refs_0_, bf16[128,1024]{1,0:T(8,128)(2,1)} %get-tuple-element.124.refs_1_, bf16[128,1024]{1,0:T(8,128)(2,1)} %copy-done.61, bf16[128,1024]{1,0:T(8,128)(2,1)} %copy-done.60, bf16[128,1024]{1,0:T(8,128)(2,1)} %collective-permute-done.18.refs_4_, ...), custom_call_target="tpu_custom_call" | custom-call | flops 4000000000 | bytes 11403296 | tf_op jit(solution)/shard_map/pallas_call | solution.py:35
  155.1 6.5 %all-to-all-start.2 = ((bf16[8,128,1792]{2,1,0:T(8,128)(2,1)}), bf16[8,128,1792]{2,1,0:T(8,128)(2,1)}, u32[]{:S(2)}, u32[]{:S(2)}) async-start(bf16[8,128,1792]{2,1,0:T(8,128)(2,1)} %shard_map.240), calls=%async_computation.4 | async-start | bytes 7340032 | tf_op jit(solution)/shard_map/all_to_all | solution.py:173
  162.5 4.7 %shard_map.241 = (f32[128,1024]{1,0:T(8,128)}, bf16[128,1024]{1,0:T(8,128)(2,1)}, f32[1,1024]{1,0:T(1,128)}, bf16[4,128,128]{2,1,0:T(8,128)(2,1)}, bf16[4,128,128]{2,1,0:T(8,128)(2,1)}) custom-call(s32[2]{0:T(128)} %pad_add_fusion.place, s32[8]{0:T(128)} %stack.89.order.refs_0_, bf16[256,1024]{1,0:T(8,128)(2,1)} %copy-done.4, ...), custom_call_target="tpu_custom_call" | custom-call | flops 300000000 | bytes 5251112 | tf_op jit(solution)/shard_map/pallas_call | solution.py:35
  178.6 11.6 %shard_map.242 = (f32[64,1]{1,0:T(8,128)}, f32[64,1]{1,0:T(8,128)}, bf16[1024,256]{1,0:T(8,128)(2,1)}, bf16[8,128,1024]{2,1,0:T(8,128)(2,1)}) custom-call(s32[8]{0:T(128)} %stack.89.order.refs_0_, bf16[1024,256]{1,0:T(8,128)(2,1)} %bitcast.74, bf16[2,128,128]{2,1,0:T(8,128)(2,1)} %pad_maximum_fusion.6.refs_2_, bf16[2,128,128]{2,1,0:T(8,128)(2,1)} %copy-done.64, ...), custom_call_target="tpu_custom_call" | custom-call | flops 8000000000 | bytes 5805088 | tf_op jit(solution)/shard_map/pallas_call | solution.py:35
  198.7 4.8 %collective-permute-start.37 = (bf16[128,1024]{1,0:T(8,128)(2,1)S(1)}, bf16[128,1024]{1,0:T(8,128)(2,1)S(1)}, u32[]{:S(2)}, u32[]{:S(2)}) collective-permute-start(bf16[128,1024]{1,0:T(8,128)(2,1)S(1)} %collective-permute-done.36.refs_14_), channel_id=1, source_target_pairs={{0,8},{8,0},{16,24},{24,16},{32,40},{40,32},{48,56},{56,48},{1,9},... | collective-permute-start | bytes 786440 | tf_op jit(solution)/shard_map/ppermute | solution.py:90
  208.3 3.2 shard_map.243
  213.9 5.9 %collective-permute-start.39 = (bf16[128,576]{1,0:T(8,128)(2,1)}, bf16[128,576]{1,0:T(8,128)(2,1)S(1)}, u32[]{:S(2)}, u32[]{:S(2)}) collective-permute-start(bf16[128,576]{1,0:T(8,128)(2,1)} %get-tuple-element.167), channel_id=1, source_target_pairs={{0,0},{1,8},{2,16},{3,24},{4,32},{5,40},{6,48},{7,56},{8,1},{9,9},... | collective-permute-start | bytes 442376 | tf_op jit(solution)/shard_map/ppermute | solution.py:127
  219.9 5.3 %shard_map.244 = bf16[8,128,512]{2,1,0:T(8,128)(2,1)} custom-call(bf16[128,1024]{1,0:T(8,128)(2,1)} %copy-done.10, bf16[128,1024]{1,0:T(8,128)(2,1)} %copy-done.24, bf16[128,1024]{1,0:T(8,128)(2,1)} %copy-done.23, bf16[128,1024]{1,0:T(8,128)(2,1)} %copy-done.27, bf16[128,1024]{1,0:T(8,128)(2,1)} %copy-done.22, bf16[128,1024]{1,0:T(8,128)(2,1)} %copy-done.26, ...), custom_call_target="tpu_custom_call" | custom-call | flops 1000000000 | bytes 6562304 | tf_op jit(solution)/shard_map/pallas_call | solution.py:35
  225.6 9.2 %collective-permute-done.39.down = bf16[128,576]{1,0:T(8,128)(2,1)S(1)} collective-permute-done((bf16[128,576]{1,0:T(8,128)(2,1)}, bf16[128,576]{1,0:T(8,128)(2,1)S(1)}, u32[]{:S(2)}, u32[]{:S(2)}) %collective-permute-start.39) | collective-permute-done | bytes 147488 | tf_op jit(solution)/shard_map/ppermute | solution.py:127
  234.8 6.4 %all-to-all-start.3 = ((bf16[8,128,512]{2,1,0:T(8,128)(2,1)}), bf16[8,128,512]{2,1,0:T(8,128)(2,1)S(1)}, u32[]{:S(2)}, u32[]{:S(2)}) async-start(bf16[8,128,512]{2,1,0:T(8,128)(2,1)} %shard_map.244), calls=%async_computation.5 | async-start | bytes 2097152 | tf_op jit(solution)/shard_map/all_to_all | solution.py:173
  245.5 11.7 %collective-permute-done.56.refs_7_ = bf16[128,1728]{1,0:T(8,128)(2,1)S(1)} collective-permute-done((bf16[128,1728]{1,0:T(8,128)(2,1)}, bf16[128,1728]{1,0:T(8,128)(2,1)S(1)}, u32[]{:S(2)}, u32[]{:S(2)}) %collective-permute-start.56) | collective-permute-done | bytes 442400 | tf_op jit(solution)/shard_map/ppermute | solution.py:94
  257.2 6.8 %collective-permute-done.54.refs_5_ = bf16[128,1728]{1,0:T(8,128)(2,1)S(1)} collective-permute-done((bf16[128,1728]{1,0:T(8,128)(2,1)}, bf16[128,1728]{1,0:T(8,128)(2,1)S(1)}, u32[]{:S(2)}, u32[]{:S(2)}) %collective-permute-start.54) | collective-permute-done | bytes 442400 | tf_op jit(solution)/shard_map/ppermute | solution.py:94
  271.3 3.7 %collective-permute-done.43.out_other = bf16[128,128]{1,0:T(8,128)(2,1)S(1)} collective-permute-done((bf16[128,128]{1,0:T(8,128)(2,1)}, bf16[128,128]{1,0:T(8,128)(2,1)S(1)}, u32[]{:S(2)}, u32[]{:S(2)}) %collective-permute-start.43) | collective-permute-done | bytes 32800 | tf_op jit(solution)/shard_map/ppermute | solution.py:127
  274.9 4.3 %collective-permute-start.42 = (bf16[128,128]{1,0:T(8,128)(2,1)}, bf16[128,128]{1,0:T(8,128)(2,1)S(1)}, u32[]{:S(2)}, u32[]{:S(2)}) collective-permute-start(bf16[128,128]{1,0:T(8,128)(2,1)} %get-tuple-element.170), channel_id=1, source_target_pairs={{0,0},{1,8},{2,16},{3,24},{4,32},{5,40},{6,48},{7,56},{8,1},{9,9},... | collective-permute-start | bytes 98312 | tf_op jit(solution)/shard_map/ppermute | solution.py:127
  279.3 3.9 %collective-permute-done.42.out = bf16[128,128]{1,0:T(8,128)(2,1)S(1)} collective-permute-done((bf16[128,128]{1,0:T(8,128)(2,1)}, bf16[128,128]{1,0:T(8,128)(2,1)S(1)}, u32[]{:S(2)}, u32[]{:S(2)}) %collective-permute-start.42) | collective-permute-done | bytes 32800 | tf_op jit(solution)/shard_map/ppermute | solution.py:127
  283.1 4.8 %collective-permute-start.53 = (bf16[128,1728]{1,0:T(8,128)(2,1)S(1)}, bf16[128,1728]{1,0:T(8,128)(2,1)}, u32[]{:S(2)}, u32[]{:S(2)}) collective-permute-start(bf16[128,1728]{1,0:T(8,128)(2,1)S(1)} %collective-permute-done.52.refs_3_), channel_id=1, source_target_pairs={{0,8},{8,0},{16,24},{24,16},{32,40},{40,32},{48,56},{56,48},{1,9},... | collective-permute-start | bytes 1327112 | tf_op jit(solution)/shard_map/ppermute | solution.py:90
  290.2 5.6 %collective-permute-start.47 = (bf16[128,512]{1,0:T(8,128)(2,1)}, bf16[128,512]{1,0:T(8,128)(2,1)S(1)}, u32[]{:S(2)}, u32[]{:S(2)}) collective-permute-start(bf16[128,512]{1,0:T(8,128)(2,1)} %shard_map.246.refs_1_), channel_id=1, source_target_pairs={{0,48},{8,56},{16,0},{24,8},{32,16},{40,24},{48,32},{56,40},{1,49}... | collective-permute-start | bytes 393224 | tf_op jit(solution)/shard_map/ppermute | solution.py:94
  305.1 6.6 %shard_map.249 = (f32[128,4608]{1,0:T(8,128)}, f32[128,4608]{1,0:T(8,128)}, f32[576,1024]{1,0:T(8,128)}) custom-call(s32[8]{0:T(128)} %stack.89.order.refs_0_, bf16[128,1728]{1,0:T(8,128)(2,1)} %shard_map.248.refs_1_, bf16[128,1728]{1,0:T(8,128)(2,1)} %collective-permute-done.51.refs_2_, bf16[128,1728]{1,0:T(8,128)(2,1)} %copy-done.19, ...), custom_call_target="tpu_custom_call" | custom-call | flops 1000000 | bytes 10616864 | tf_op jit(solution)/shard_map/pallas_call | solution.py:35
  312.5 3.3 shard_map.247
  (293 shorter events, 106.2 us)
Async XLA Ops:
  9.9 25.0 %all-to-all-start = ((bf16[8,128,256]{2,1,0:T(8,128)(2,1)}), bf16[8,128,256]{2,1,0:T(8,128)(2,1)S(1)}, u32[]{:S(2)}, u32[]{:S(2)}) async-start(bf16[8,128,256]{2,1,0:T(8,128)(2,1)} %broadcast_in_dim.20), calls=%async_computation | async-start | bytes 1048576 | tf_op jit(solution)/shard_map/all_to_all | solution.py:173
  16.5 105.2 %all-gather.2.cloned.1.call-start = ((), (), s32[]{:S(2)}) async-start(), calls=%async_computation.6 | async-start | bytes 4128768 | tf_op jit(solution)/shard_map/all_gather | solution.py:520
  16.8 17.0 %collective-permute-start.7 = (bf16[128,576]{1,0:T(8,128)(2,1)S(1)}, bf16[128,576]{1,0:T(8,128)(2,1)S(1)}, u32[]{:S(2)}, u32[]{:S(2)}) collective-permute-start(bf16[128,576]{1,0:T(8,128)(2,1)S(1)} %bitcast.79), channel_id=1, source_target_pairs={{0,0},{1,8},{2,16},{3,24},{4,32},{5,40},{6,48},{7,56},{8,1},{9,9},... | collective-permute-start | bytes 442376 | tf_op jit(solution)/shard_map/ppermute | solution.py:127
  38.2 14.1 %collective-permute-start = (bf16[128,1024]{1,0:T(8,128)(2,1)S(1)}, bf16[128,1024]{1,0:T(8,128)(2,1)S(1)}, u32[]{:S(2)}, u32[]{:S(2)}) collective-permute-start(bf16[128,1024]{1,0:T(8,128)(2,1)S(1)} %fusion.3.refs_0_), channel_id=1, source_target_pairs={{0,8},{8,0},{16,24},{24,16},{32,40},{40,32},{48,56},{56,48},{1,9},... | collective-permute-start | bytes 786440 | tf_op jit(solution)/shard_map/ppermute | solution.py:90
  56.7 42.3 %collective-permute-start.15 = (bf16[256,1024]{1,0:T(8,128)(2,1)S(1)}, bf16[256,1024]{1,0:T(8,128)(2,1)S(1)}, u32[]{:S(2)}, u32[]{:S(2)}) collective-permute-start(bf16[256,1024]{1,0:T(8,128)(2,1)S(1)} %pad_maximum_fusion.refs_0_), channel_id=1, source_target_pairs={{0,4},{1,5},{2,6},{3,7},{4,0},{5,1},{6,2},{7,3},{8,12},{9,13},{10,... | collective-permute-start | bytes 1572872 | tf_op jit(solution)/shard_map/ppermute | solution.py:136
  56.8 42.2 %collective-permute-start.14 = (bf16[256,1024]{1,0:T(8,128)(2,1)S(1)}, bf16[256,1024]{1,0:T(8,128)(2,1)}, u32[]{:S(2)}, u32[]{:S(2)}) collective-permute-start(bf16[256,1024]{1,0:T(8,128)(2,1)S(1)} %pad_maximum_fusion.refs_0_), channel_id=1, source_target_pairs={{0,6},{1,7},{2,0},{3,1},{4,2},{5,3},{6,4},{7,5},{8,14},{9,15},{10,... | collective-permute-start | bytes 1572872 | tf_op jit(solution)/shard_map/ppermute | solution.py:136
  59.4 39.7 %collective-permute-start.13 = (bf16[256,1024]{1,0:T(8,128)(2,1)S(1)}, bf16[256,1024]{1,0:T(8,128)(2,1)}, u32[]{:S(2)}, u32[]{:S(2)}) collective-permute-start(bf16[256,1024]{1,0:T(8,128)(2,1)S(1)} %pad_maximum_fusion.refs_0_), channel_id=1, source_target_pairs={{0,2},{1,3},{2,4},{3,5},{4,6},{5,7},{6,0},{7,1},{8,10},{9,11},{10,... | collective-permute-start | bytes 1572872 | tf_op jit(solution)/shard_map/ppermute | solution.py:136
  59.6 62.2 %all-to-all-start.1 = ((bf16[8,128,1024]{2,1,0:T(8,128)(2,1)}), bf16[8,128,1024]{2,1,0:T(8,128)(2,1)S(1)}, u32[]{:S(2)}, u32[]{:S(2)}) async-start(bf16[8,128,1024]{2,1,0:T(8,128)(2,1)} %broadcast_in_dim.23), calls=%async_computation.1 | async-start | bytes 4194304 | tf_op jit(solution)/shard_map/all_to_all | solution.py:173
  66.3 237.1 %reduce-scatter.3.cloned.1.call-start = ((), (), s32[]{:S(2)}) async-start(), calls=%async_computation.7 | async-start | bytes 2359296 | tf_op jit(solution)/shard_map/reduce_scatter | solution.py:577
  80.1 13.9 %collective-permute-start.10 = (bf16[2,128,128]{2,1,0:T(8,128)(2,1)S(1)}, bf16[2,128,128]{2,1,0:T(8,128)(2,1)S(1)}, u32[]{:S(2)}, u32[]{:S(2)}) collective-permute-start(bf16[2,128,128]{2,1,0:T(8,128)(2,1)S(1)} %pad_maximum_fusion.3), channel_id=1, source_target_pairs={{0,16},{8,24},{16,32},{24,40},{32,48},{40,56},{48,0},{56,8},{1,17}... | collective-permute-start | bytes 196616 | tf_op jit(solution)/shard_map/ppermute | solution.py:94
  81.5 13.6 %collective-permute-start.11 = (bf16[2,128,128]{2,1,0:T(8,128)(2,1)S(1)}, bf16[2,128,128]{2,1,0:T(8,128)(2,1)S(1)}, u32[]{:S(2)}, u32[]{:S(2)}) collective-permute-start(bf16[2,128,128]{2,1,0:T(8,128)(2,1)S(1)} %pad_maximum_fusion.4), channel_id=1, source_target_pairs={{0,48},{8,56},{16,0},{24,8},{32,16},{40,24},{48,32},{56,40},{1,49}... | collective-permute-start | bytes 196616 | tf_op jit(solution)/shard_map/ppermute | solution.py:94
  105.5 14.1 %collective-permute-start.17 = (bf16[128,1024]{1,0:T(8,128)(2,1)}, bf16[128,1024]{1,0:T(8,128)(2,1)S(1)}, u32[]{:S(2)}, u32[]{:S(2)}) collective-permute-start(bf16[128,1024]{1,0:T(8,128)(2,1)} %get-tuple-element.124.refs_1_), channel_id=1, source_target_pairs={{0,16},{8,24},{16,32},{24,40},{32,48},{40,56},{48,0},{56,8},{1,17}... | collective-permute-start | bytes 786440 | tf_op jit(solution)/shard_map/ppermute | solution.py:94
  105.9 14.5 %collective-permute-start.16 = (bf16[128,1024]{1,0:T(8,128)(2,1)}, bf16[128,1024]{1,0:T(8,128)(2,1)S(1)}, u32[]{:S(2)}, u32[]{:S(2)}) collective-permute-start(bf16[128,1024]{1,0:T(8,128)(2,1)} %get-tuple-element.124.refs_1_), channel_id=1, source_target_pairs={{0,8},{8,0},{16,24},{24,16},{32,40},{40,32},{48,56},{56,48},{1,9},... | collective-permute-start | bytes 786440 | tf_op jit(solution)/shard_map/ppermute | solution.py:90
  142.6 19.1 %collective-permute-start.26 = (bf16[128,1024]{1,0:T(8,128)(2,1)}, bf16[128,1024]{1,0:T(8,128)(2,1)S(1)}, u32[]{:S(2)}, u32[]{:S(2)}) collective-permute-start(bf16[128,1024]{1,0:T(8,128)(2,1)} %get-tuple-element.183), channel_id=1, source_target_pairs={{0,16},{8,24},{16,32},{24,40},{32,48},{40,56},{48,0},{56,8},{1,17}... | collective-permute-start | bytes 786440 | tf_op jit(solution)/shard_map/ppermute | solution.py:94
  142.6 19.1 %collective-permute-start.25 = (bf16[128,1024]{1,0:T(8,128)(2,1)}, bf16[128,1024]{1,0:T(8,128)(2,1)S(1)}, u32[]{:S(2)}, u32[]{:S(2)}) collective-permute-start(bf16[128,1024]{1,0:T(8,128)(2,1)} %get-tuple-element.184), channel_id=1, source_target_pairs={{0,48},{8,56},{16,0},{24,8},{32,16},{40,24},{48,32},{56,40},{1,49}... | collective-permute-start | bytes 786440 | tf_op jit(solution)/shard_map/ppermute | solution.py:94
  145.2 16.4 %collective-permute-start.24 = (bf16[128,1024]{1,0:T(8,128)(2,1)S(1)}, bf16[128,1024]{1,0:T(8,128)(2,1)S(1)}, u32[]{:S(2)}, u32[]{:S(2)}) collective-permute-start(bf16[128,1024]{1,0:T(8,128)(2,1)S(1)} %get-tuple-element.185), channel_id=1, source_target_pairs={{0,32},{8,40},{16,48},{24,56},{32,0},{40,8},{48,16},{56,24},{1,33}... | collective-permute-start | bytes 786440 | tf_op jit(solution)/shard_map/ppermute | solution.py:94
  155.1 53.2 %all-to-all-start.2 = ((bf16[8,128,1792]{2,1,0:T(8,128)(2,1)}), bf16[8,128,1792]{2,1,0:T(8,128)(2,1)}, u32[]{:S(2)}, u32[]{:S(2)}) async-start(bf16[8,128,1792]{2,1,0:T(8,128)(2,1)} %shard_map.240), calls=%async_computation.4 | async-start | bytes 7340032 | tf_op jit(solution)/shard_map/all_to_all | solution.py:173
  161.6 156.8 %reduce-scatter.5.cloned.1.call-start = ((), (), s32[]{:S(2)}) async-start(), calls=%async_computation.8 | async-start | bytes 2359296 | tf_op jit(solution)/shard_map/reduce_scatter | solution.py:614
  194.5 17.0 %collective-permute-start.31 = (bf16[128,1024]{1,0:T(8,128)(2,1)S(1)}, bf16[128,1024]{1,0:T(8,128)(2,1)S(1)}, u32[]{:S(2)}, u32[]{:S(2)}) collective-permute-start(bf16[128,1024]{1,0:T(8,128)(2,1)S(1)} %copy-done.28), channel_id=1, source_target_pairs={{0,8},{8,0},{16,24},{24,16},{32,40},{40,32},{48,56},{56,48},{1,9},... | collective-permute-start | bytes 786440 | tf_op jit(solution)/shard_map/ppermute | solution.py:90
  211.6 23.2 %collective-permute-start.38 = (bf16[128,1152]{1,0:T(8,128)(2,1)}, bf16[128,1152]{1,0:T(8,128)(2,1)S(1)}, u32[]{:S(2)}, u32[]{:S(2)}) collective-permute-start(bf16[128,1152]{1,0:T(8,128)(2,1)} %get-tuple-element.176.own), channel_id=1, source_target_pairs={{0,64},{64,0},{1,65},{65,1},{2,66},{66,2},{3,67},{67,3},{4,68},{68... | collective-permute-start | bytes 884744 | tf_op jit(solution)/shard_map/ppermute | solution.py:131
  213.9 20.9 %collective-permute-start.39 = (bf16[128,576]{1,0:T(8,128)(2,1)}, bf16[128,576]{1,0:T(8,128)(2,1)S(1)}, u32[]{:S(2)}, u32[]{:S(2)}) collective-permute-start(bf16[128,576]{1,0:T(8,128)(2,1)} %get-tuple-element.167), channel_id=1, source_target_pairs={{0,0},{1,8},{2,16},{3,24},{4,32},{5,40},{6,48},{7,56},{8,1},{9,9},... | collective-permute-start | bytes 442376 | tf_op jit(solution)/shard_map/ppermute | solution.py:127
  234.8 30.0 %all-to-all-start.3 = ((bf16[8,128,512]{2,1,0:T(8,128)(2,1)}), bf16[8,128,512]{2,1,0:T(8,128)(2,1)S(1)}, u32[]{:S(2)}, u32[]{:S(2)}) async-start(bf16[8,128,512]{2,1,0:T(8,128)(2,1)} %shard_map.244), calls=%async_computation.5 | async-start | bytes 2097152 | tf_op jit(solution)/shard_map/all_to_all | solution.py:173
  243.2 13.9 %collective-permute-start.56 = (bf16[128,1728]{1,0:T(8,128)(2,1)}, bf16[128,1728]{1,0:T(8,128)(2,1)S(1)}, u32[]{:S(2)}, u32[]{:S(2)}) collective-permute-start(bf16[128,1728]{1,0:T(8,128)(2,1)} %shard_map.248.refs_1_), channel_id=1, source_target_pairs={{0,32},{8,40},{16,48},{24,56},{32,0},{40,8},{48,16},{56,24},{1,33}... | collective-permute-start | bytes 1327112 | tf_op jit(solution)/shard_map/ppermute | solution.py:94
  243.2 20.7 %collective-permute-start.54 = (bf16[128,1728]{1,0:T(8,128)(2,1)}, bf16[128,1728]{1,0:T(8,128)(2,1)S(1)}, u32[]{:S(2)}, u32[]{:S(2)}) collective-permute-start(bf16[128,1728]{1,0:T(8,128)(2,1)} %shard_map.248.refs_1_), channel_id=1, source_target_pairs={{0,48},{8,56},{16,0},{24,8},{32,16},{40,24},{48,32},{56,40},{1,49}... | collective-permute-start | bytes 1327112 | tf_op jit(solution)/shard_map/ppermute | solution.py:94
  245.5 24.3 %collective-permute-start.52 = (bf16[128,1728]{1,0:T(8,128)(2,1)}, bf16[128,1728]{1,0:T(8,128)(2,1)S(1)}, u32[]{:S(2)}, u32[]{:S(2)}) collective-permute-start(bf16[128,1728]{1,0:T(8,128)(2,1)} %shard_map.248.refs_1_), channel_id=1, source_target_pairs={{0,16},{8,24},{16,32},{24,40},{32,48},{40,56},{48,0},{56,8},{1,17}... | collective-permute-start | bytes 1327112 | tf_op jit(solution)/shard_map/ppermute | solution.py:94
  245.5 44.7 %collective-permute-start.51 = (bf16[128,1728]{1,0:T(8,128)(2,1)}, bf16[128,1728]{1,0:T(8,128)(2,1)}, u32[]{:S(2)}, u32[]{:S(2)}) collective-permute-start(bf16[128,1728]{1,0:T(8,128)(2,1)} %shard_map.248.refs_1_), channel_id=1, source_target_pairs={{0,8},{8,0},{16,24},{24,16},{32,40},{40,32},{48,56},{56,48},{1,9},... | collective-permute-start | bytes 1327112 | tf_op jit(solution)/shard_map/ppermute | solution.py:90
  257.2 38.7 %collective-permute-start.57 = (bf16[128,1728]{1,0:T(8,128)(2,1)S(1)}, bf16[128,1728]{1,0:T(8,128)(2,1)}, u32[]{:S(2)}, u32[]{:S(2)}) collective-permute-start(bf16[128,1728]{1,0:T(8,128)(2,1)S(1)} %collective-permute-done.56.refs_7_), channel_id=1, source_target_pairs={{0,8},{8,0},{16,24},{24,16},{32,40},{40,32},{48,56},{56,48},{1,9},... | collective-permute-start | bytes 1327112 | tf_op jit(solution)/shard_map/ppermute | solution.py:90
  264.0 31.9 %collective-permute-start.55 = (bf16[128,1728]{1,0:T(8,128)(2,1)S(1)}, bf16[128,1728]{1,0:T(8,128)(2,1)}, u32[]{:S(2)}, u32[]{:S(2)}) collective-permute-start(bf16[128,1728]{1,0:T(8,128)(2,1)S(1)} %collective-permute-done.54.refs_5_), channel_id=1, source_target_pairs={{0,8},{8,0},{16,24},{24,16},{32,40},{40,32},{48,56},{56,48},{1,9},... | collective-permute-start | bytes 1327112 | tf_op jit(solution)/shard_map/ppermute | solution.py:90
  269.8 18.2 %collective-permute-start.41 = (bf16[128,384]{1,0:T(8,128)(2,1)}, bf16[128,384]{1,0:T(8,128)(2,1)S(1)}, u32[]{:S(2)}, u32[]{:S(2)}) collective-permute-start(bf16[128,384]{1,0:T(8,128)(2,1)} %get-tuple-element.169.own), channel_id=1, source_target_pairs={{0,64},{64,0},{1,65},{65,1},{2,66},{66,2},{3,67},{67,3},{4,68},{68... | collective-permute-start | bytes 294920 | tf_op jit(solution)/shard_map/ppermute | solution.py:131
  283.1 22.0 %collective-permute-start.53 = (bf16[128,1728]{1,0:T(8,128)(2,1)S(1)}, bf16[128,1728]{1,0:T(8,128)(2,1)}, u32[]{:S(2)}, u32[]{:S(2)}) collective-permute-start(bf16[128,1728]{1,0:T(8,128)(2,1)S(1)} %collective-permute-done.52.refs_3_), channel_id=1, source_target_pairs={{0,8},{8,0},{16,24},{24,16},{32,40},{40,32},{48,56},{56,48},{1,9},... | collective-permute-start | bytes 1327112 | tf_op jit(solution)/shard_map/ppermute | solution.py:90
  295.8 15.9 %collective-permute-start.44 = (bf16[128,512]{1,0:T(8,128)(2,1)}, bf16[128,512]{1,0:T(8,128)(2,1)S(1)}, u32[]{:S(2)}, u32[]{:S(2)}) collective-permute-start(bf16[128,512]{1,0:T(8,128)(2,1)} %shard_map.246.refs_1_), channel_id=1, source_target_pairs={{0,8},{8,0},{16,24},{24,16},{32,40},{40,32},{48,56},{56,48},{1,9},... | collective-permute-start | bytes 393224 | tf_op jit(solution)/shard_map/ppermute | solution.py:90
  297.1 14.7 %collective-permute-start.50 = (bf16[128,512]{1,0:T(8,128)(2,1)S(1)}, bf16[128,512]{1,0:T(8,128)(2,1)S(1)}, u32[]{:S(2)}, u32[]{:S(2)}) collective-permute-start(bf16[128,512]{1,0:T(8,128)(2,1)S(1)} %collective-permute-done.49.refs_7_), channel_id=1, source_target_pairs={{0,8},{8,0},{16,24},{24,16},{32,40},{40,32},{48,56},{56,48},{1,9},... | collective-permute-start | bytes 393224 | tf_op jit(solution)/shard_map/ppermute | solution.py:90
  (100 other events, 998.6 us)
Sparse Core Ops, SparseCore 0:
  35.0 75.0 all-gather.1
  138.5 37.2 reduce-scatter.2
  190.3 39.5 reduce-scatter.4
where the time goes:
time: 334 us; the launch traced here: 328 us
  starting transfers between devices  115 us (34%)
  waiting for transfers between devices  82.5 us (25%)
  Pallas kernels  81.3 us (24%)
  local copies, waits for them, and re-layouts  23.8 us (7%)
  between operations  14.9 us (4%)
  other arithmetic  10.6 us (3%)
    pallas_call x13, Pallas kernels, call(): pl.pallas_call(kernel, out_shape=out_shapes, in_specs=[pl.BlockSpec(memor...  81.3 us
    ppermute x24, waiting for transfers between devices, move_z(): lax.ppermute(value, 'ctx', [(i, (i + 2 * step) % 8) for i in range(8)])  49.4 us
    ppermute x23, starting transfers between devices, swap_core(): return lax.ppermute(value, 'ctx', [(i, i ^ 1) for i in range(8)])  35.5 us
    ppermute x24, starting transfers between devices, move_z(): lax.ppermute(value, 'ctx', [(i, (i + 2 * step) % 8) for i in range(8)])  27.4 us
    ppermute x5, waiting for transfers between devices, transpose_mesh(): return lax.ppermute(value, ('dp', 'ctx', 'fsdp'), pairs)  27.4 us
    all_to_all x4, starting transfers between devices, all_to_all(): return lax.all_to_all(blocks, axis, split_axis=0, concat_axis=0, tiled=True)  26.3 us
    ppermute x5, starting transfers between devices, transpose_mesh(): return lax.ppermute(value, ('dp', 'ctx', 'fsdp'), pairs)  19.1 us
    unnamed x135, local copies, waits for them, and re-layouts  9.31 us
  transfers between devices with their start and end apart: 65, of which 23 were waited for; matrix products, arithmetic and copies ran while one was open for 6% of the time, Pallas kernels for 20%

commit v1 on v0

--- a/solution.py
+++ b/solution.py
@@ -94,12 +94,19 @@
     return lax.ppermute(value, "ctx", [(i, (i + 2 * step) % 8) for i in range(8)])
 
 
+def move_pieces(block):
+    return [move_z(block, -step) if step else block for step in STEPS]
+
+
+def swap_pieces(moved):
+    pieces = []
+    for piece in moved:
+        pieces += [piece, swap_core(piece)]
+    return pieces
+
+
 def gather_ctx(block):
-    pieces = []
-    for step in STEPS:
-        mine = block if step == 0 else move_z(block, -step)
-        pieces += [mine, swap_core(mine)]
-    return pieces
+    return swap_pieces(move_pieces(block))
 
 
 def start_scatter_ctx(mine, received):
@@ -503,7 +510,7 @@
     first_scale = rms_scale(tokens)
     first_hat = tokens * first_scale
     first_normed = (first_hat * attn_gain).astype(BF16)
-    first_pieces = gather_ctx(first_normed)
+    first_moved = move_pieces(first_normed)
     qkv_block = jnp.concatenate(
         [own_columns(w_query, q_width, ctx), own_columns(w_key, k_width, ctx), own_columns(w_value, k_width, ctx)],
         axis=1,
@@ -516,11 +523,12 @@
     ffn_block = jnp.concatenate(
         [own_columns(w_gate, ff_width, ctx), own_columns(w_up, ff_width, ctx), down_chunk], axis=1
     )
-    ffn_block, w_qkv = stage(ffn_block, w_qkv)
+    ffn_block, w_qkv, first_moved, cot_copies = stage(ffn_block, w_qkv, first_moved, cot_copies)
     ffn_rows = lax.all_gather(ffn_block, "fsdp", axis=0, tiled=True)
-    first_pieces, w_qkv, tables, out_pair, cot_copies = stage(first_pieces, w_qkv, tables, out_pair, cot_copies)
-
     cots = all_to_all(cot_copies, "ctx")
+    first_pieces = swap_pieces(first_moved)
+    first_pieces, w_qkv, tables, out_pair = stage(first_pieces, w_qkv, tables, out_pair)
+
     out_pairs = spread_y(out_pair)
     qkv, lse, own, other = call(
         attend_forward,
@@ -534,7 +542,7 @@
     )
 
     mixed_blocks = exchange_ctx(own, other)
-    mixed_blocks, out_pairs = stage(mixed_blocks, out_pairs)
+    mixed_blocks, out_pairs, cots = stage(mixed_blocks, out_pairs, cots)
     square = pltpu.VMEM((width, width), BF16)
     residual, second_normed = call(
         out_project,
@@ -590,7 +598,7 @@
     d_blocks = exchange_ctx(*d_blocks)
     d_blocks, d_attn = stage(d_blocks, d_attn)
 
-    d_pieces = gather_ctx(d_attn)
+    d_moved = move_pieces(d_attn)
     q_gain_part, k_gain_part, d_qkv, d_first_parts = call(
         attend_backward,
         [
@@ -606,6 +614,8 @@
         [pltpu.VMEM((qkv_width, length), F32), pltpu.VMEM((width, qkv_width), BF16)],
         1,
     )
+    d_qkv, d_first_parts, d_moved = stage(d_qkv, d_first_parts, d_moved)
+    d_pieces = swap_pieces(d_moved)
     half, down = call(
         sum_ffn, [shape((count, 2 * ff_width), BF16), shape((count, ff_width), BF16)], (), (), (ffn_sums,), 10**6
     )
@@ -622,47 +632,41 @@
         [wide, wide, pltpu.VMEM((length, q_width), BF16), head_rows, pltpu.VMEM((width, qkv_width), BF16)],
         26,
     )
-    attn_partial, ffn_steps = stage(attn_partial, ffn_steps)
-
+    (joined,) = call(join_ffn, [shape((count, 3 * ff_width), BF16)], (), (), ffn_steps, 10**6)
+    attn_partial, joined = stage(attn_partial, joined)
+
+    ffn_moved = move_pieces(joined)
     attn_sums = all_to_all(attn_partial, "fsdp")
-    (joined,) = call(
-        join_ffn,
-        [shape((count, 3 * ff_width), BF16)],
-        (),
-        (),
-        ffn_steps,
-        10**6,
-    )
-    ffn_parts = gather_ctx(joined)
+    d_from_first, _ = norm_back(d_first, first_hat, first_scale, attn_gain)
+    grad_in = (d_resid + d_from_first).astype(BF16)
+    attn_sums, ffn_moved, grad_in, block_out = stage(attn_sums, ffn_moved, grad_in, block_out)
     half, out = call(
         sum_attn, [shape((count, qkv_width + 128), BF16), shape((count, q_width), BF16)], (), (), (attn_sums,), 10**6
     )
+    attn_steps = (half, swap_dp(half), transpose_mesh(out), transpose_mesh(out, 1))
     (joined,) = call(
-        join_attn,
-        [shape((count, qkv_width + 128 + q_width), BF16)],
-        (),
-        (),
-        (half, swap_dp(half), transpose_mesh(out), transpose_mesh(out, 1)),
-        10**6,
-    )
-    attn_parts = gather_ctx(joined)
-    d_from_first, _ = norm_back(d_first, first_hat, first_scale, attn_gain)
-    grad_in = (d_resid + d_from_first).astype(BF16)
-    grad_gate, grad_up, grad_down = call(
+        join_attn, [shape((count, qkv_width + 128 + q_width), BF16)], (), (), attn_steps, 10**6
+    )
+    attn_moved = move_pieces(joined)
+    grads_ffn = call(
         assemble_ffn,
         [shape((count, 8 * ff_width), F32)] * 2 + [shape((ff_width, width), F32)],
         (owners,),
-        ffn_parts,
+        swap_pieces(ffn_moved),
         (),
         10**6,
         [pltpu.VMEM((8, count, 3 * ff_width), BF16)],
         8,
     )
+    attn_moved, grads_ffn = stage(attn_moved, grads_ffn)
+    grad_gate, grad_up, grad_down = grads_ffn
     grad_query, grad_key, grad_value, grad_out, totals = call(
         assemble_attn,
-        [shape((count, width), F32)] + [shape((count, 8 * k_width), F32)] * 2 + [shape((q_width, width), F32), shape((24, 128), F32)],
+        [shape((count, width), F32)]
+        + [shape((count, 8 * k_width), F32)] * 2
+        + [shape((q_width, width), F32), shape((24, 128), F32)],
         (owners,),
-        attn_parts,
+        swap_pieces(attn_moved),
         (),
         10**6,
         [pltpu.VMEM((8, count, qkv_width + 128 + q_width), BF16)],

time: 334 us -> 360 us (1.078)
  the two profiles are of different devices: /device:TPU:31 before, /device:TPU:7 now
where the time goes in v1:
time: 360 us; the launch traced here: 354 us
  starting transfers between devices  116 us (32%)
  waiting for transfers between devices  113 us (31%)
  Pallas kernels  81.1 us (23%)
  local copies, waits for them, and re-layouts  19.6 us (5%)
  between operations  14.9 us (4%)
  other arithmetic  9.55 us (3%)
    pallas_call x13, Pallas kernels, call(): pl.pallas_call(kernel, out_shape=out_shapes, in_specs=[pl.BlockSpec(memor...  81.1 us
    ppermute x24, waiting for transfers between devices, move_z(): lax.ppermute(value, 'ctx', [(i, (i + 2 * step) % 8) for i in range(8)])  50.4 us
    all_to_all x4, starting transfers between devices, all_to_all(): return lax.all_to_all(blocks, axis, split_axis=0, concat_axis=0, tiled=True)  41.9 us
    ppermute x24, starting transfers between devices, move_z(): lax.ppermute(value, 'ctx', [(i, (i + 2 * step) % 8) for i in range(8)])  40.4 us
    all_to_all x4, waiting for transfers between devices, all_to_all(): return lax.all_to_all(blocks, axis, split_axis=0, concat_axis=0, tiled=True)  37.2 us
    ppermute x23, starting transfers between devices, swap_core(): return lax.ppermute(value, 'ctx', [(i, i ^ 1) for i in range(8)])  22.1 us
    all_gather x1, waiting for transfers between devices, body(): ffn_rows = lax.all_gather(ffn_block, 'fsdp', axis=0, tiled=True)  7.75 us
    ppermute x23, waiting for transfers between devices, swap_core(): return lax.ppermute(value, 'ctx', [(i, i ^ 1) for i in range(8)])  7.44 us
  transfers between devices with their start and end apart: 65, of which 33 were waited for; matrix products, arithmetic and copies ran while one was open for 5% of the time, Pallas kernels for 18%

profile of v1, /device:TPU:7, one launch (start us, length us, event | category | flops | bytes accessed | tf_op | source)
XLA Modules:
  0.0 353.7 jit_solution(3056883833905763371)
XLA Ops:
  9.9 7.0 %all-to-all-start = ((bf16[8,128,256]{2,1,0:T(8,128)(2,1)}), bf16[8,128,256]{2,1,0:T(8,128)(2,1)S(1)}, u32[]{:S(2)}, u32[]{:S(2)}) async-start(bf16[8,128,256]{2,1,0:T(8,128)(2,1)} %broadcast_in_dim.20), calls=%async_computation | async-start | bytes 1048576 | tf_op jit(solution)/shard_map/all_to_all | solution.py:180
  17.2 3.7 %collective-permute-start.3 = (bf16[128,1024]{1,0:T(8,128)(2,1)S(1)}, bf16[128,1024]{1,0:T(8,128)(2,1)S(1)}, u32[]{:S(2)}, u32[]{:S(2)}) collective-permute-start(bf16[128,1024]{1,0:T(8,128)(2,1)S(1)} %fusion.3.refs_0_), channel_id=1, source_target_pairs={{0,32},{8,40},{16,48},{24,56},{32,0},{40,8},{48,16},{56,24},{1,33}... | collective-permute-start | bytes 786440 | tf_op jit(solution)/shard_map/ppermute | solution.py:94
  26.3 10.0 %collective-permute-done.2.refs_4_ = bf16[128,1024]{1,0:T(8,128)(2,1)S(1)} collective-permute-done((bf16[128,1024]{1,0:T(8,128)(2,1)S(1)}, bf16[128,1024]{1,0:T(8,128)(2,1)S(1)}, u32[]{:S(2)}, u32[]{:S(2)}) %collective-permute-start.2) | collective-permute-done | bytes 262176 | tf_op jit(solution)/shard_map/ppermute | solution.py:94
  40.7 6.4 %all-to-all-start.1 = ((bf16[8,128,1024]{2,1,0:T(8,128)(2,1)}), bf16[8,128,1024]{2,1,0:T(8,128)(2,1)}, u32[]{:S(2)}, u32[]{:S(2)}) async-start(bf16[8,128,1024]{2,1,0:T(8,128)(2,1)} %broadcast_in_dim.22), calls=%async_computation.1 | async-start | bytes 4194304 | tf_op jit(solution)/shard_map/all_to_all | solution.py:180
  54.8 3.4 collective-permute-start.15
  60.4 11.9 %shard_map.237 = (f32[256,1024]{1,0:T(8,128)}, f32[8,1024]{1,0:T(8,128)}, bf16[4,128,128]{2,1,0:T(8,128)(2,1)}, bf16[4,128,128]{2,1,0:T(8,128)(2,1)}) custom-call(bf16[128,1024]{1,0:T(8,128)(2,1)} %copy-done.12, bf16[128,1024]{1,0:T(8,128)(2,1)} %copy-done.27, bf16[128,1024]{1,0:T(8,128)(2,1)} %copy-done.26, bf16[128,1024]{1,0:T(8,128)(2,1)} %copy-done.28, ...), custom_call_target="tpu_custom_call" | custom-call | flops 4000000000 | bytes 5280256 | tf_op jit(solution)/shard_map/pallas_call | solution.py:35
  83.9 3.2 collective-permute-done.14.refs_2_
  88.0 4.1 %shard_map.238 = (f32[128,1024]{1,0:T(8,128)}, bf16[128,1024]{1,0:T(8,128)(2,1)}) custom-call(s32[2]{0:T(128)} %pad_add_fusion.place, s32[8]{0:T(128)} %stack.95.order.refs_0_, bf16[256,1024]{1,0:T(8,128)(2,1)} %copy-done.4, bf16[256,1024]{1,0:T(8,128)(2,1)} %copy-done.9, bf16[256,1024]{1,0:T(8,128)(2,1)} %copy-done.8, bf16[256,1024]{1,0:T(8,128)(2,1)} %copy-done.7, ...), custom_call_target="tpu_custom_call" | custom-call | flops 300000000 | bytes 3412008 | tf_op jit(solution)/shard_map/pallas_call | solution.py:35
  92.2 2.8 collective-permute-start.21
  97.9 3.6 %collective-permute-done.21.refs_7_ = bf16[128,1024]{1,0:T(8,128)(2,1)S(1)} collective-permute-done((bf16[128,1024]{1,0:T(8,128)(2,1)}, bf16[128,1024]{1,0:T(8,128)(2,1)S(1)}, u32[]{:S(2)}, u32[]{:S(2)}) %collective-permute-start.21) | collective-permute-done | bytes 262176 | tf_op jit(solution)/shard_map/ppermute | solution.py:94
  103.6 3.7 %collective-permute-done.19.refs_5_ = bf16[128,1024]{1,0:T(8,128)(2,1)S(1)} collective-permute-done((bf16[128,1024]{1,0:T(8,128)(2,1)}, bf16[128,1024]{1,0:T(8,128)(2,1)S(1)}, u32[]{:S(2)}, u32[]{:S(2)}) %collective-permute-start.19) | collective-permute-done | bytes 262176 | tf_op jit(solution)/shard_map/ppermute | solution.py:94
  110.3 7.8 %all-gather.2.cloned.1.call-done.refs_10_ = bf16[1024,1728]{1,0:T(8,128)(2,1)} async-done(((bf16[128,1728]{1,0:T(8,128)(2,1)}), bf16[1024,1728]{1,0:T(8,128)(2,1)}) %all-gather.2.cloned.1.call-update) | async-done | bytes 3538960 | tf_op jit(solution)/shard_map/all_gather | solution.py:527
  118.1 15.3 %shard_map.239 = (bf16[1024,576]{1,0:T(8,128)(2,1)}, bf16[1024,1152]{1,0:T(8,128)(2,1)}, bf16[8,128,1024]{2,1,0:T(8,128)(2,1)}, bf16[4,128,1024]{2,1,0:T(8,128)(...) custom-call(s32[8]{0:T(128)} %stack.95.order.refs_0_, ...), custom_call_target="tpu_custom_call" | custom-call | flops 8000000000 | bytes 16515104 | tf_op jit(solution)/shard_map/pallas_call | solution.py:35
  143.1 9.7 %shard_map.240 = bf16[8,128,1792]{2,1,0:T(8,128)(2,1)} custom-call(s32[8]{0:T(128)} %stack.95.order.refs_0_, bf16[128,1024]{1,0:T(8,128)(2,1)} %get-tuple-element.150.refs_1_, bf16[128,1024]{1,0:T(8,128)(2,1)} %copy-done.67, bf16[128,1024]{1,0:T(8,128)(2,1)} %copy-done.66, bf16[128,1024]{1,0:T(8,128)(2,1)} %copy-done.70, bf16[128,1024]{1,0:T(8,128)(2,1)} %copy-done.65, ...), custom_call_target="tpu_custom_call" | custom-call | flops 4000000000 | bytes 11403296 | tf_op jit(solution)/shard_map/pallas_call | solution.py:35
  152.8 5.0 %collective-permute-done.24.refs_5_ = bf16[128,1024]{1,0:T(8,128)(2,1)S(1)} collective-permute-done((bf16[128,1024]{1,0:T(8,128)(2,1)S(1)}, bf16[128,1024]{1,0:T(8,128)(2,1)S(1)}, u32[]{:S(2)}, u32[]{:S(2)}) %collective-permute-start.24) | collective-permute-done | bytes 262176 | tf_op jit(solution)/shard_map/ppermute | solution.py:94
  158.5 4.7 %shard_map.241 = (f32[128,1024]{1,0:T(8,128)}, bf16[128,1024]{1,0:T(8,128)(2,1)}, f32[1,1024]{1,0:T(1,128)}, bf16[4,128,128]{2,1,0:T(8,128)(2,1)}, bf16[4,128,128]{2,1,0:T(8,128)(2,1)}) custom-call(s32[2]{0:T(128)} %pad_add_fusion.place, s32[8]{0:T(128)} %stack.95.order.refs_0_, bf16[256,1024]{1,0:T(8,128)(2,1)} %copy-done.4, bf16[256,1024]{1,0:T(8,128)(2,1)} %copy-done.9, ...), custom_call_target="tpu_custom_call" | custom-call | flops 300000000 | bytes 5251112 | tf_op jit(solution)/shard_map/pallas_call | solution.py:35
  176.5 11.6 %shard_map.242 = (f32[64,1]{1,0:T(8,128)}, f32[64,1]{1,0:T(8,128)}, bf16[1024,256]{1,0:T(8,128)(2,1)}, bf16[8,128,1024]{2,1,0:T(8,128)(2,1)}) custom-call(s32[8]{0:T(128)} %stack.95.order.refs_0_, bf16[1024,256]{1,0:T(8,128)(2,1)} %bitcast.72, bf16[2,128,128]{2,1,0:T(8,128)(2,1)} %pad_maximum_fusion.6.refs_2_, bf16[2,128,128]{2,1,0:T(8,128)(2,1)} %copy-done.71, ...), custom_call_target="tpu_custom_call" | custom-call | flops 8000000000 | bytes 5805088 | tf_op jit(solution)/shard_map/pallas_call | solution.py:35
  188.4 6.7 %all-to-all-start.2 = ((bf16[8,128,1792]{2,1,0:T(8,128)(2,1)}), bf16[8,128,1792]{2,1,0:T(8,128)(2,1)}, u32[]{:S(2)}, u32[]{:S(2)}) async-start(bf16[8,128,1792]{2,1,0:T(8,128)(2,1)} %shard_map.240), calls=%async_computation.2 | async-start | bytes 7340032 | tf_op jit(solution)/shard_map/all_to_all | solution.py:180
  195.0 2.8 collective-permute-start.34
  198.4 37.2 %all-to-all-done.2.parts = bf16[8,128,1792]{2,1,0:T(8,128)(2,1)} async-done(((bf16[8,128,1792]{2,1,0:T(8,128)(2,1)}), bf16[8,128,1792]{2,1,0:T(8,128)(2,1)}, u32[]{:S(2)}, u32[]{:S(2)}) %all-to-all-start.2) | async-done | bytes 3670048 | tf_op jit(solution)/shard_map/all_to_all | solution.py:180
  235.6 3.2 shard_map.243
  242.2 5.3 %shard_map.244 = bf16[8,128,512]{2,1,0:T(8,128)(2,1)} custom-call(bf16[128,1024]{1,0:T(8,128)(2,1)} %copy-done.12, bf16[128,1024]{1,0:T(8,128)(2,1)} %copy-done.27, bf16[128,1024]{1,0:T(8,128)(2,1)} %copy-done.26, bf16[128,1024]{1,0:T(8,128)(2,1)} %copy-done.28, bf16[128,1024]{1,0:T(8,128)(2,1)} %copy-done.25, bf16[128,1024]{1,0:T(8,128)(2,1)} %copy-done.29, ...), custom_call_target="tpu_custom_call" | custom-call | flops 1000000000 | bytes 6562304 | tf_op jit(solution)/shard_map/pallas_call | solution.py:35
  251.2 21.8 %all-to-all-start.3 = ((bf16[8,128,512]{2,1,0:T(8,128)(2,1)}), bf16[8,128,512]{2,1,0:T(8,128)(2,1)S(1)}, u32[]{:S(2)}, u32[]{:S(2)}) async-start(bf16[8,128,512]{2,1,0:T(8,128)(2,1)} %shard_map.244), calls=%async_computation.3 | async-start | bytes 2097152 | tf_op jit(solution)/shard_map/all_to_all | solution.py:180
  279.4 7.5 %collective-permute-done.43.refs_7_ = bf16[128,1728]{1,0:T(8,128)(2,1)S(1)} collective-permute-done((bf16[128,1728]{1,0:T(8,128)(2,1)S(1)}, bf16[128,1728]{1,0:T(8,128)(2,1)S(1)}, u32[]{:S(2)}, u32[]{:S(2)}) %collective-permute-start.43) | collective-permute-done | bytes 442400 | tf_op jit(solution)/shard_map/ppermute | solution.py:94
  286.9 5.6 %collective-permute-done.42.refs_5_ = bf16[128,1728]{1,0:T(8,128)(2,1)} collective-permute-done((bf16[128,1728]{1,0:T(8,128)(2,1)S(1)}, bf16[128,1728]{1,0:T(8,128)(2,1)}, u32[]{:S(2)}, u32[]{:S(2)}) %collective-permute-start.42) | collective-permute-done | bytes 442400 | tf_op jit(solution)/shard_map/ppermute | solution.py:94
  292.5 4.4 %collective-permute-done.41.refs_3_ = bf16[128,1728]{1,0:T(8,128)(2,1)} collective-permute-done((bf16[128,1728]{1,0:T(8,128)(2,1)S(1)}, bf16[128,1728]{1,0:T(8,128)(2,1)}, u32[]{:S(2)}, u32[]{:S(2)}) %collective-permute-start.41) | collective-permute-done | bytes 442400 | tf_op jit(solution)/shard_map/ppermute | solution.py:94
  300.0 3.0 collective-permute-done.46.out_other
  304.7 3.4 collective-permute-done.44.other
  310.4 12.8 %collective-permute-start.49 = (bf16[128,512]{1,0:T(8,128)(2,1)}, bf16[128,512]{1,0:T(8,128)(2,1)S(1)}, u32[]{:S(2)}, u32[]{:S(2)}) collective-permute-start(bf16[128,512]{1,0:T(8,128)(2,1)} %shard_map.247.refs_1_), channel_id=1, source_target_pairs={{0,32},{8,40},{16,48},{24,56},{32,0},{40,8},{48,16},{56,24},{1,33}... | collective-permute-start | bytes 393224 | tf_op jit(solution)/shard_map/ppermute | solution.py:94
  324.7 6.4 %shard_map.248 = (f32[128,4608]{1,0:T(8,128)}, f32[128,4608]{1,0:T(8,128)}, f32[576,1024]{1,0:T(8,128)}) custom-call(s32[8]{0:T(128)} %stack.95.order.refs_0_, bf16[128,1728]{1,0:T(8,128)(2,1)} %shard_map.245.refs_1_, bf16[128,1728]{1,0:T(8,128)(2,1)} %copy-done.21, bf16[128,1728]{1,0:T(8,128)(2,1)} %collective-permute-done.41.refs_3_, ...), custom_call_target="tpu_custom_call" | custom-call | flops 1000000 | bytes 10616864 | tf_op jit(solution)/shard_map/pallas_call | solution.py:35
  331.2 7.0 %collective-permute-start.54 = (bf16[128,512]{1,0:T(8,128)(2,1)S(1)}, bf16[128,512]{1,0:T(8,128)(2,1)S(1)}, u32[]{:S(2)}, u32[]{:S(2)}) collective-permute-start(bf16[128,512]{1,0:T(8,128)(2,1)S(1)} %copy-done.19), channel_id=1, source_target_pairs={{0,8},{8,0},{16,24},{24,16},{32,40},{40,32},{48,56},{56,48},{1,9},... | collective-permute-start | bytes 393224 | tf_op jit(solution)/shard_map/ppermute | solution.py:90
  341.0 3.3 shard_map.249
  (307 shorter events, 94.8 us)
Async XLA Ops:
  9.9 28.1 %all-to-all-start = ((bf16[8,128,256]{2,1,0:T(8,128)(2,1)}), bf16[8,128,256]{2,1,0:T(8,128)(2,1)S(1)}, u32[]{:S(2)}, u32[]{:S(2)}) async-start(bf16[8,128,256]{2,1,0:T(8,128)(2,1)} %broadcast_in_dim.20), calls=%async_computation | async-start | bytes 1048576 | tf_op jit(solution)/shard_map/all_to_all | solution.py:180
  16.9 101.2 %all-gather.2.cloned.1.call-start = ((), (), s32[]{:S(2)}) async-start(), calls=%async_computation.6 | async-start | bytes 4128768 | tf_op jit(solution)/shard_map/all_gather | solution.py:527
  20.9 15.4 %collective-permute-start.2 = (bf16[128,1024]{1,0:T(8,128)(2,1)S(1)}, bf16[128,1024]{1,0:T(8,128)(2,1)S(1)}, u32[]{:S(2)}, u32[]{:S(2)}) collective-permute-start(bf16[128,1024]{1,0:T(8,128)(2,1)S(1)} %fusion.3.refs_0_), channel_id=1, source_target_pairs={{0,48},{8,56},{16,0},{24,8},{32,16},{40,24},{48,32},{56,40},{1,49}... | collective-permute-start | bytes 786440 | tf_op jit(solution)/shard_map/ppermute | solution.py:94
  21.3 16.6 %collective-permute-start.1 = (bf16[128,1024]{1,0:T(8,128)(2,1)S(1)}, bf16[128,1024]{1,0:T(8,128)(2,1)S(1)}, u32[]{:S(2)}, u32[]{:S(2)}) collective-permute-start(bf16[128,1024]{1,0:T(8,128)(2,1)S(1)} %fusion.3.refs_0_), channel_id=1, source_target_pairs={{0,16},{8,24},{16,32},{24,40},{32,48},{40,56},{48,0},{56,8},{1,17}... | collective-permute-start | bytes 786440 | tf_op jit(solution)/shard_map/ppermute | solution.py:94
  40.7 46.4 %all-to-all-start.1 = ((bf16[8,128,1024]{2,1,0:T(8,128)(2,1)}), bf16[8,128,1024]{2,1,0:T(8,128)(2,1)}, u32[]{:S(2)}, u32[]{:S(2)}) async-start(bf16[8,128,1024]{2,1,0:T(8,128)(2,1)} %broadcast_in_dim.22), calls=%async_computation.1 | async-start | bytes 4194304 | tf_op jit(solution)/shard_map/all_to_all | solution.py:180
  47.1 227.5 %reduce-scatter.5.cloned.1.call-start = ((), (), s32[]{:S(2)}) async-start(), calls=%async_computation.8 | async-start | bytes 2359296 | tf_op jit(solution)/shard_map/reduce_scatter | solution.py:585
  54.8 29.1 %collective-permute-start.15 = (bf16[256,1024]{1,0:T(8,128)(2,1)S(1)}, bf16[256,1024]{1,0:T(8,128)(2,1)S(1)}, u32[]{:S(2)}, u32[]{:S(2)}) collective-permute-start(bf16[256,1024]{1,0:T(8,128)(2,1)S(1)} %pad_maximum_fusion.refs_0_), channel_id=1, source_target_pairs={{0,4},{1,5},{2,6},{3,7},{4,0},{5,1},{6,2},{7,3},{8,12},{9,13},{10,... | collective-permute-start | bytes 1572872 | tf_op jit(solution)/shard_map/ppermute | solution.py:143
  58.2 28.8 %collective-permute-start.14 = (bf16[256,1024]{1,0:T(8,128)(2,1)S(1)}, bf16[256,1024]{1,0:T(8,128)(2,1)S(1)}, u32[]{:S(2)}, u32[]{:S(2)}) collective-permute-start(bf16[256,1024]{1,0:T(8,128)(2,1)S(1)} %pad_maximum_fusion.refs_0_), channel_id=1, source_target_pairs={{0,6},{1,7},{2,0},{3,1},{4,2},{5,3},{6,4},{7,5},{8,14},{9,15},{10,... | collective-permute-start | bytes 1572872 | tf_op jit(solution)/shard_map/ppermute | solution.py:143
  60.2 26.9 %collective-permute-start.13 = (bf16[256,1024]{1,0:T(8,128)(2,1)S(1)}, bf16[256,1024]{1,0:T(8,128)(2,1)S(1)}, u32[]{:S(2)}, u32[]{:S(2)}) collective-permute-start(bf16[256,1024]{1,0:T(8,128)(2,1)S(1)} %pad_maximum_fusion.refs_0_), channel_id=1, source_target_pairs={{0,2},{1,3},{2,4},{3,5},{4,6},{5,7},{6,0},{7,1},{8,10},{9,11},{10,... | collective-permute-start | bytes 1572872 | tf_op jit(solution)/shard_map/ppermute | solution.py:143
  94.9 12.4 %collective-permute-start.19 = (bf16[128,1024]{1,0:T(8,128)(2,1)}, bf16[128,1024]{1,0:T(8,128)(2,1)S(1)}, u32[]{:S(2)}, u32[]{:S(2)}) collective-permute-start(bf16[128,1024]{1,0:T(8,128)(2,1)} %get-tuple-element.150.refs_1_), channel_id=1, source_target_pairs={{0,48},{8,56},{16,0},{24,8},{32,16},{40,24},{48,32},{56,40},{1,49}... | collective-permute-start | bytes 786440 | tf_op jit(solution)/shard_map/ppermute | solution.py:94
  95.7 12.9 %collective-permute-start.17 = (bf16[128,1024]{1,0:T(8,128)(2,1)}, bf16[128,1024]{1,0:T(8,128)(2,1)S(1)}, u32[]{:S(2)}, u32[]{:S(2)}) collective-permute-start(bf16[128,1024]{1,0:T(8,128)(2,1)} %get-tuple-element.150.refs_1_), channel_id=1, source_target_pairs={{0,16},{8,24},{16,32},{24,40},{32,48},{40,56},{48,0},{56,8},{1,17}... | collective-permute-start | bytes 786440 | tf_op jit(solution)/shard_map/ppermute | solution.py:94
  96.4 12.5 %collective-permute-start.16 = (bf16[128,1024]{1,0:T(8,128)(2,1)}, bf16[128,1024]{1,0:T(8,128)(2,1)S(1)}, u32[]{:S(2)}, u32[]{:S(2)}) collective-permute-start(bf16[128,1024]{1,0:T(8,128)(2,1)} %get-tuple-element.150.refs_1_), channel_id=1, source_target_pairs={{0,8},{8,0},{16,24},{24,16},{32,40},{40,32},{48,56},{56,48},{1,9},... | collective-permute-start | bytes 786440 | tf_op jit(solution)/shard_map/ppermute | solution.py:90
  133.4 142.8 %reduce-scatter.3.cloned.1.call-start = ((), (), s32[]{:S(2)}) async-start(), calls=%async_computation.7 | async-start | bytes 2359296 | tf_op jit(solution)/shard_map/reduce_scatter | solution.py:624
  138.3 14.4 %collective-permute-start.26 = (bf16[128,1024]{1,0:T(8,128)(2,1)S(1)}, bf16[128,1024]{1,0:T(8,128)(2,1)S(1)}, u32[]{:S(2)}, u32[]{:S(2)}) collective-permute-start(bf16[128,1024]{1,0:T(8,128)(2,1)S(1)} %get-tuple-element.227), channel_id=1, source_target_pairs={{0,16},{8,24},{16,32},{24,40},{32,48},{40,56},{48,0},{56,8},{1,17}... | collective-permute-start | bytes 786440 | tf_op jit(solution)/shard_map/ppermute | solution.py:94
  139.6 13.1 %collective-permute-start.25 = (bf16[128,1024]{1,0:T(8,128)(2,1)S(1)}, bf16[128,1024]{1,0:T(8,128)(2,1)S(1)}, u32[]{:S(2)}, u32[]{:S(2)}) collective-permute-start(bf16[128,1024]{1,0:T(8,128)(2,1)S(1)} %get-tuple-element.228), channel_id=1, source_target_pairs={{0,48},{8,56},{16,0},{24,8},{32,16},{40,24},{48,32},{56,40},{1,49}... | collective-permute-start | bytes 786440 | tf_op jit(solution)/shard_map/ppermute | solution.py:94
  141.0 16.8 %collective-permute-start.24 = (bf16[128,1024]{1,0:T(8,128)(2,1)S(1)}, bf16[128,1024]{1,0:T(8,128)(2,1)S(1)}, u32[]{:S(2)}, u32[]{:S(2)}) collective-permute-start(bf16[128,1024]{1,0:T(8,128)(2,1)S(1)} %get-tuple-element.229), channel_id=1, source_target_pairs={{0,32},{8,40},{16,48},{24,56},{32,0},{40,8},{48,16},{56,24},{1,33}... | collective-permute-start | bytes 786440 | tf_op jit(solution)/shard_map/ppermute | solution.py:94
  173.9 14.2 %collective-permute-start.33 = (bf16[128,1024]{1,0:T(8,128)(2,1)}, bf16[128,1024]{1,0:T(8,128)(2,1)S(1)}, u32[]{:S(2)}, u32[]{:S(2)}) collective-permute-start(bf16[128,1024]{1,0:T(8,128)(2,1)} %get-tuple-element.184.refs_8_), channel_id=1, source_target_pairs={{0,32},{8,40},{16,48},{24,56},{32,0},{40,8},{48,16},{56,24},{1,33}... | collective-permute-start | bytes 786440 | tf_op jit(solution)/shard_map/ppermute | solution.py:94
  174.2 13.9 %collective-permute-start.32 = (bf16[128,1024]{1,0:T(8,128)(2,1)}, bf16[128,1024]{1,0:T(8,128)(2,1)S(1)}, u32[]{:S(2)}, u32[]{:S(2)}) collective-permute-start(bf16[128,1024]{1,0:T(8,128)(2,1)} %get-tuple-element.184.refs_8_), channel_id=1, source_target_pairs={{0,48},{8,56},{16,0},{24,8},{32,16},{40,24},{48,32},{56,40},{1,49}... | collective-permute-start | bytes 786440 | tf_op jit(solution)/shard_map/ppermute | solution.py:94
  188.4 47.3 %all-to-all-start.2 = ((bf16[8,128,1792]{2,1,0:T(8,128)(2,1)}), bf16[8,128,1792]{2,1,0:T(8,128)(2,1)}, u32[]{:S(2)}, u32[]{:S(2)}) async-start(bf16[8,128,1792]{2,1,0:T(8,128)(2,1)} %shard_map.240), calls=%async_computation.2 | async-start | bytes 7340032 | tf_op jit(solution)/shard_map/all_to_all | solution.py:180
  195.0 43.8 %collective-permute-start.34 = (bf16[128,1024]{1,0:T(8,128)(2,1)S(1)}, bf16[128,1024]{1,0:T(8,128)(2,1)S(1)}, u32[]{:S(2)}, u32[]{:S(2)}) collective-permute-start(bf16[128,1024]{1,0:T(8,128)(2,1)S(1)} %copy-done.31), channel_id=1, source_target_pairs={{0,8},{8,0},{16,24},{24,16},{32,40},{40,32},{48,56},{56,48},{1,9},... | collective-permute-start | bytes 786440 | tf_op jit(solution)/shard_map/ppermute | solution.py:90
  197.8 41.0 %collective-permute-start.35 = (bf16[128,1024]{1,0:T(8,128)(2,1)S(1)}, bf16[128,1024]{1,0:T(8,128)(2,1)S(1)}, u32[]{:S(2)}, u32[]{:S(2)}) collective-permute-start(bf16[128,1024]{1,0:T(8,128)(2,1)S(1)} %collective-permute-done.31.refs_10_), channel_id=1, source_target_pairs={{0,8},{8,0},{16,24},{24,16},{32,40},{40,32},{48,56},{56,48},{1,9},... | collective-permute-start | bytes 786440 | tf_op jit(solution)/shard_map/ppermute | solution.py:90
  197.9 40.9 %collective-permute-start.36 = (bf16[128,1024]{1,0:T(8,128)(2,1)S(1)}, bf16[128,1024]{1,0:T(8,128)(2,1)S(1)}, u32[]{:S(2)}, u32[]{:S(2)}) collective-permute-start(bf16[128,1024]{1,0:T(8,128)(2,1)S(1)} %collective-permute-done.32.refs_12_), channel_id=1, source_target_pairs={{0,8},{8,0},{16,24},{24,16},{32,40},{40,32},{48,56},{56,48},{1,9},... | collective-permute-start | bytes 786440 | tf_op jit(solution)/shard_map/ppermute | solution.py:90
  198.3 40.5 %collective-permute-start.37 = (bf16[128,1024]{1,0:T(8,128)(2,1)S(1)}, bf16[128,1024]{1,0:T(8,128)(2,1)S(1)}, u32[]{:S(2)}, u32[]{:S(2)}) collective-permute-start(bf16[128,1024]{1,0:T(8,128)(2,1)S(1)} %collective-permute-done.33.refs_14_), channel_id=1, source_target_pairs={{0,8},{8,0},{16,24},{24,16},{32,40},{40,32},{48,56},{56,48},{1,9},... | collective-permute-start | bytes 786440 | tf_op jit(solution)/shard_map/ppermute | solution.py:90
  251.2 45.7 %all-to-all-start.3 = ((bf16[8,128,512]{2,1,0:T(8,128)(2,1)}), bf16[8,128,512]{2,1,0:T(8,128)(2,1)S(1)}, u32[]{:S(2)}, u32[]{:S(2)}) async-start(bf16[8,128,512]{2,1,0:T(8,128)(2,1)} %shard_map.244), calls=%async_computation.3 | async-start | bytes 2097152 | tf_op jit(solution)/shard_map/all_to_all | solution.py:180
  273.0 13.9 %collective-permute-start.43 = (bf16[128,1728]{1,0:T(8,128)(2,1)S(1)}, bf16[128,1728]{1,0:T(8,128)(2,1)S(1)}, u32[]{:S(2)}, u32[]{:S(2)}) collective-permute-start(bf16[128,1728]{1,0:T(8,128)(2,1)S(1)} %copy-done.11), channel_id=1, source_target_pairs={{0,32},{8,40},{16,48},{24,56},{32,0},{40,8},{48,16},{56,24},{1,33}... | collective-permute-start | bytes 1327112 | tf_op jit(solution)/shard_map/ppermute | solution.py:94
  273.0 19.5 %collective-permute-start.42 = (bf16[128,1728]{1,0:T(8,128)(2,1)S(1)}, bf16[128,1728]{1,0:T(8,128)(2,1)}, u32[]{:S(2)}, u32[]{:S(2)}) collective-permute-start(bf16[128,1728]{1,0:T(8,128)(2,1)S(1)} %copy-done.11), channel_id=1, source_target_pairs={{0,48},{8,56},{16,0},{24,8},{32,16},{40,24},{48,32},{56,40},{1,49}... | collective-permute-start | bytes 1327112 | tf_op jit(solution)/shard_map/ppermute | solution.py:94
  274.4 22.5 %collective-permute-start.41 = (bf16[128,1728]{1,0:T(8,128)(2,1)S(1)}, bf16[128,1728]{1,0:T(8,128)(2,1)}, u32[]{:S(2)}, u32[]{:S(2)}) collective-permute-start(bf16[128,1728]{1,0:T(8,128)(2,1)S(1)} %copy-done.11), channel_id=1, source_target_pairs={{0,16},{8,24},{16,32},{24,40},{32,48},{40,56},{48,0},{56,8},{1,17}... | collective-permute-start | bytes 1327112 | tf_op jit(solution)/shard_map/ppermute | solution.py:94
  296.9 26.3 %collective-permute-start.50 = (bf16[128,1728]{1,0:T(8,128)(2,1)S(1)}, bf16[128,1728]{1,0:T(8,128)(2,1)S(1)}, u32[]{:S(2)}, u32[]{:S(2)}) collective-permute-start(bf16[128,1728]{1,0:T(8,128)(2,1)S(1)} %copy-done.11), channel_id=1, source_target_pairs={{0,8},{8,0},{16,24},{24,16},{32,40},{40,32},{48,56},{56,48},{1,9},... | collective-permute-start | bytes 1327112 | tf_op jit(solution)/shard_map/ppermute | solution.py:90
  297.4 25.8 %collective-permute-start.51 = (bf16[128,1728]{1,0:T(8,128)(2,1)}, bf16[128,1728]{1,0:T(8,128)(2,1)S(1)}, u32[]{:S(2)}, u32[]{:S(2)}) collective-permute-start(bf16[128,1728]{1,0:T(8,128)(2,1)} %collective-permute-done.41.refs_3_), channel_id=1, source_target_pairs={{0,8},{8,0},{16,24},{24,16},{32,40},{40,32},{48,56},{56,48},{1,9},... | collective-permute-start | bytes 1327112 | tf_op jit(solution)/shard_map/ppermute | solution.py:90
  297.5 27.2 %collective-permute-start.52 = (bf16[128,1728]{1,0:T(8,128)(2,1)}, bf16[128,1728]{1,0:T(8,128)(2,1)}, u32[]{:S(2)}, u32[]{:S(2)}) collective-permute-start(bf16[128,1728]{1,0:T(8,128)(2,1)} %collective-permute-done.42.refs_5_), channel_id=1, source_target_pairs={{0,8},{8,0},{16,24},{24,16},{32,40},{40,32},{48,56},{56,48},{1,9},... | collective-permute-start | bytes 1327112 | tf_op jit(solution)/shard_map/ppermute | solution.py:90
  297.9 26.7 %collective-permute-start.53 = (bf16[128,1728]{1,0:T(8,128)(2,1)S(1)}, bf16[128,1728]{1,0:T(8,128)(2,1)}, u32[]{:S(2)}, u32[]{:S(2)}) collective-permute-start(bf16[128,1728]{1,0:T(8,128)(2,1)S(1)} %collective-permute-done.43.refs_7_), channel_id=1, source_target_pairs={{0,8},{8,0},{16,24},{24,16},{32,40},{40,32},{48,56},{56,48},{1,9},... | collective-permute-start | bytes 1327112 | tf_op jit(solution)/shard_map/ppermute | solution.py:90
  310.4 20.7 %collective-permute-start.49 = (bf16[128,512]{1,0:T(8,128)(2,1)}, bf16[128,512]{1,0:T(8,128)(2,1)S(1)}, u32[]{:S(2)}, u32[]{:S(2)}) collective-permute-start(bf16[128,512]{1,0:T(8,128)(2,1)} %shard_map.247.refs_1_), channel_id=1, source_target_pairs={{0,32},{8,40},{16,48},{24,56},{32,0},{40,8},{48,16},{56,24},{1,33}... | collective-permute-start | bytes 393224 | tf_op jit(solution)/shard_map/ppermute | solution.py:94
  (107 other events, 879.7 us)
Sparse Core Ops, SparseCore 0:
  39.7 78.3 all-gather.1
  133.6 36.5 reduce-scatter.4
  188.5 31.9 reduce-scatter.2

commit v2 on v1

--- a/solution.py
+++ b/solution.py
@@ -523,8 +523,8 @@
     ffn_block = jnp.concatenate(
         [own_columns(w_gate, ff_width, ctx), own_columns(w_up, ff_width, ctx), down_chunk], axis=1
     )
-    ffn_block, w_qkv, first_moved, cot_copies = stage(ffn_block, w_qkv, first_moved, cot_copies)
     ffn_rows = lax.all_gather(ffn_block, "fsdp", axis=0, tiled=True)
+    w_qkv, first_moved, cot_copies = stage(w_qkv, first_moved, cot_copies)
     cots = all_to_all(cot_copies, "ctx")
     first_pieces = swap_pieces(first_moved)
     first_pieces, w_qkv, tables, out_pair = stage(first_pieces, w_qkv, tables, out_pair)
@@ -598,7 +598,7 @@
     d_blocks = exchange_ctx(*d_blocks)
     d_blocks, d_attn = stage(d_blocks, d_attn)
 
-    d_moved = move_pieces(d_attn)
+    d_pieces = gather_ctx(d_attn)
     q_gain_part, k_gain_part, d_qkv, d_first_parts = call(
         attend_backward,
         [
@@ -614,8 +614,6 @@
         [pltpu.VMEM((qkv_width, length), F32), pltpu.VMEM((width, qkv_width), BF16)],
         1,
     )
-    d_qkv, d_first_parts, d_moved = stage(d_qkv, d_first_parts, d_moved)
-    d_pieces = swap_pieces(d_moved)
     half, down = call(
         sum_ffn, [shape((count, 2 * ff_width), BF16), shape((count, ff_width), BF16)], (), (), (ffn_sums,), 10**6
     )
@@ -639,7 +637,7 @@
     attn_sums = all_to_all(attn_partial, "fsdp")
     d_from_first, _ = norm_back(d_first, first_hat, first_scale, attn_gain)
     grad_in = (d_resid + d_from_first).astype(BF16)
-    attn_sums, ffn_moved, grad_in, block_out = stage(attn_sums, ffn_moved, grad_in, block_out)
+    attn_sums, grad_in, block_out = stage(attn_sums, grad_in, block_out)
     half, out = call(
         sum_attn, [shape((count, qkv_width + 128), BF16), shape((count, q_width), BF16)], (), (), (attn_sums,), 10**6
     )
@@ -647,6 +645,7 @@
     (joined,) = call(
         join_attn, [shape((count, qkv_width + 128 + q_width), BF16)], (), (), attn_steps, 10**6
     )
+    joined, ffn_moved = stage(joined, ffn_moved)
     attn_moved = move_pieces(joined)
     grads_ffn = call(
         assemble_ffn,

time: 360 us -> 352 us (0.978)
  the two profiles are of different devices: /device:TPU:7 before, /device:TPU:1 now
where the time goes in v2:
time: 352 us; the launch traced here: 346 us
  starting transfers between devices  119 us (34%)
  waiting for transfers between devices  94.7 us (27%)
  Pallas kernels  81.5 us (23%)
  local copies, waits for them, and re-layouts  24.9 us (7%)
  between operations  14.9 us (4%)
  other arithmetic  10.6 us (3%)
    pallas_call x13, Pallas kernels, call(): pl.pallas_call(kernel, out_shape=out_shapes, in_specs=[pl.BlockSpec(memor...  81.5 us
    all_to_all x4, waiting for transfers between devices, all_to_all(): return lax.all_to_all(blocks, axis, split_axis=0, concat_axis=0, tiled=True)  45.1 us
    ppermute x24, starting transfers between devices, move_z(): lax.ppermute(value, 'ctx', [(i, (i + 2 * step) % 8) for i in range(8)])  40.9 us
    all_to_all x4, starting transfers between devices, all_to_all(): return lax.all_to_all(blocks, axis, split_axis=0, concat_axis=0, tiled=True)  30 us
    ppermute x23, starting transfers between devices, swap_core(): return lax.ppermute(value, 'ctx', [(i, i ^ 1) for i in range(8)])  27.2 us
    ppermute x24, waiting for transfers between devices, move_z(): lax.ppermute(value, 'ctx', [(i, (i + 2 * step) % 8) for i in range(8)])  23.7 us
    ppermute x5, starting transfers between devices, transpose_mesh(): return lax.ppermute(value, ('dp', 'ctx', 'fsdp'), pairs)  16.6 us
    unnamed x147, local copies, waits for them, and re-layouts  10.5 us
  transfers between devices with their start and end apart: 65, of which 28 were waited for; matrix products, arithmetic and copies ran while one was open for 6% of the time, Pallas kernels for 18%

profile of v2, /device:TPU:1, one launch (start us, length us, event | category | flops | bytes accessed | tf_op | source)
XLA Modules:
  0.0 345.9 jit_solution(11889126918400310680)
XLA Ops:
  8.7 6.0 %collective-permute-start.22 = (bf16[128,576]{1,0:T(8,128)(2,1)S(1)}, bf16[128,576]{1,0:T(8,128)(2,1)S(1)}, u32[]{:S(2)}, u32[]{:S(2)}) collective-permute-start(bf16[128,576]{1,0:T(8,128)(2,1)S(1)} %bitcast.79), channel_id=1, source_target_pairs={{0,0},{1,8},{2,16},{3,24},{4,32},{5,40},{6,48},{7,56},{8,1},{9,9},... | collective-permute-start | bytes 442376 | tf_op jit(solution)/shard_map/ppermute | solution.py:134
  19.0 10.2 %collective-permute-start.2 = (bf16[128,1024]{1,0:T(8,128)(2,1)S(1)}, bf16[128,1024]{1,0:T(8,128)(2,1)S(1)}, u32[]{:S(2)}, u32[]{:S(2)}) collective-permute-start(bf16[128,1024]{1,0:T(8,128)(2,1)S(1)} %fusion.3.refs_0_), channel_id=1, source_target_pairs={{0,32},{8,40},{16,48},{24,56},{32,0},{40,8},{48,16},{56,24},{1,33}... | collective-permute-start | bytes 786440 | tf_op jit(solution)/shard_map/ppermute | solution.py:94
  35.1 3.5 %all-to-all-start = ((bf16[8,128,256]{2,1,0:T(8,128)(2,1)}), bf16[8,128,256]{2,1,0:T(8,128)(2,1)S(1)}, u32[]{:S(2)}, u32[]{:S(2)}) async-start(bf16[8,128,256]{2,1,0:T(8,128)(2,1)} %broadcast_in_dim.20), calls=%async_computation | async-start | bytes 1048576 | tf_op jit(solution)/shard_map/all_to_all | solution.py:180
  40.4 10.6 %all-to-all-done = bf16[8,128,256]{2,1,0:T(8,128)(2,1)S(1)} async-done(((bf16[8,128,256]{2,1,0:T(8,128)(2,1)}), bf16[8,128,256]{2,1,0:T(8,128)(2,1)S(1)}, u32[]{:S(2)}, u32[]{:S(2)}) %all-to-all-start) | async-done | bytes 524320 | tf_op jit(solution)/shard_map/all_to_all | solution.py:180
  52.6 6.1 %all-to-all-start.1 = ((bf16[8,128,1024]{2,1,0:T(8,128)(2,1)}), bf16[8,128,1024]{2,1,0:T(8,128)(2,1)S(1)}, u32[]{:S(2)}, u32[]{:S(2)}) async-start(bf16[8,128,1024]{2,1,0:T(8,128)(2,1)} %broadcast_in_dim.22), calls=%async_computation.1 | async-start | bytes 4194304 | tf_op jit(solution)/shard_map/all_to_all | solution.py:180
  68.8 11.9 %shard_map.237 = (f32[256,1024]{1,0:T(8,128)}, f32[8,1024]{1,0:T(8,128)}, bf16[4,128,128]{2,1,0:T(8,128)(2,1)}, bf16[4,128,128]{2,1,0:T(8,128)(2,1)}) custom-call(bf16[128,1024]{1,0:T(8,128)(2,1)} %copy-done.12, bf16[128,1024]{1,0:T(8,128)(2,1)} %copy-done.28, bf16[128,1024]{1,0:T(8,128)(2,1)} %copy-done.27, bf16[128,1024]{1,0:T(8,128)(2,1)} %copy-done.29, ...), custom_call_target="tpu_custom_call" | custom-call | flops 4000000000 | bytes 5280256 | tf_op jit(solution)/shard_map/pallas_call | solution.py:35
  92.7 9.4 %collective-permute-done.13.refs_2_ = bf16[256,1024]{1,0:T(8,128)(2,1)S(1)} collective-permute-done((bf16[256,1024]{1,0:T(8,128)(2,1)S(1)}, bf16[256,1024]{1,0:T(8,128)(2,1)S(1)}, u32[]{:S(2)}, u32[]{:S(2)}) %collective-permute-start.13) | collective-permute-done | bytes 524320 | tf_op jit(solution)/shard_map/ppermute | solution.py:143
  103.4 4.6 %shard_map.238 = (f32[128,1024]{1,0:T(8,128)}, bf16[128,1024]{1,0:T(8,128)(2,1)}) custom-call(s32[2]{0:T(128)} %pad_add_fusion.place, s32[8]{0:T(128)} %stack.95.order.refs_0_, bf16[256,1024]{1,0:T(8,128)(2,1)} %copy-done.4, bf16[256,1024]{1,0:T(8,128)(2,1)} %collective-permute-done.12.refs_1_, bf16[256,1024]{1,0:T(8,128)(2,1)} %copy-done.9, ...), custom_call_target="tpu_custom_call" | custom-call | flops 300000000 | bytes 3412008 | tf_op jit(solution)/shard_map/pallas_call | solution.py:35
  107.9 2.9 collective-permute-start.20
  113.8 3.2 collective-permute-done.20.refs_7_
  119.5 3.4 collective-permute-done.18.refs_5_
  126.5 15.3 %shard_map.239 = (bf16[1024,576]{1,0:T(8,128)(2,1)}, bf16[1024,1152]{1,0:T(8,128)(2,1)}, bf16[8,128,1024]{2,1,0:T(8,128)(2,1)}, bf16[4,128,1024]{2,1,0:T(8,128)(...) custom-call(s32[8]{0:T(128)} %stack.95.order.refs_0_, ...), custom_call_target="tpu_custom_call" | custom-call | flops 8000000000 | bytes 16515104 | tf_op jit(solution)/shard_map/pallas_call | solution.py:35
  149.6 9.7 %shard_map.240 = bf16[8,128,1792]{2,1,0:T(8,128)(2,1)} custom-call(s32[8]{0:T(128)} %stack.95.order.refs_0_, bf16[128,1024]{1,0:T(8,128)(2,1)} %get-tuple-element.144.refs_1_, bf16[128,1024]{1,0:T(8,128)(2,1)} %copy-done.67, bf16[128,1024]{1,0:T(8,128)(2,1)} %copy-done.66, bf16[128,1024]{1,0:T(8,128)(2,1)} %collective-permute-done.17.refs_4_, ...), custom_call_target="tpu_custom_call" | custom-call | flops 4000000000 | bytes 11403296 | tf_op jit(solution)/shard_map/pallas_call | solution.py:35
  159.3 5.8 %collective-permute-done.24.refs_5_ = bf16[128,1024]{1,0:T(8,128)(2,1)S(1)} collective-permute-done((bf16[128,1024]{1,0:T(8,128)(2,1)S(1)}, bf16[128,1024]{1,0:T(8,128)(2,1)S(1)}, u32[]{:S(2)}, u32[]{:S(2)}) %collective-permute-start.24) | collective-permute-done | bytes 262176 | tf_op jit(solution)/shard_map/ppermute | solution.py:94
  165.9 4.7 %shard_map.241 = (f32[128,1024]{1,0:T(8,128)}, bf16[128,1024]{1,0:T(8,128)(2,1)}, f32[1,1024]{1,0:T(1,128)}, bf16[4,128,128]{2,1,0:T(8,128)(2,1)}, bf16[4,128,128]{2,1,0:T(8,128)(2,1)}) custom-call(s32[2]{0:T(128)} %pad_add_fusion.place, s32[8]{0:T(128)} %stack.95.order.refs_0_, bf16[256,1024]{1,0:T(8,128)(2,1)} %copy-done.4, ...), custom_call_target="tpu_custom_call" | custom-call | flops 300000000 | bytes 5251112 | tf_op jit(solution)/shard_map/pallas_call | solution.py:35
  181.6 11.6 %shard_map.242 = (f32[64,1]{1,0:T(8,128)}, f32[64,1]{1,0:T(8,128)}, bf16[1024,256]{1,0:T(8,128)(2,1)}, bf16[8,128,1024]{2,1,0:T(8,128)(2,1)}) custom-call(s32[8]{0:T(128)} %stack.95.order.refs_0_, bf16[1024,256]{1,0:T(8,128)(2,1)} %bitcast.72, bf16[2,128,128]{2,1,0:T(8,128)(2,1)} %pad_maximum_fusion.6.refs_2_, bf16[2,128,128]{2,1,0:T(8,128)(2,1)} %copy-done.70, ...), custom_call_target="tpu_custom_call" | custom-call | flops 8000000000 | bytes 5805088 | tf_op jit(solution)/shard_map/pallas_call | solution.py:35
  193.3 5.4 %all-to-all-start.2 = ((bf16[8,128,1792]{2,1,0:T(8,128)(2,1)}), bf16[8,128,1792]{2,1,0:T(8,128)(2,1)}, u32[]{:S(2)}, u32[]{:S(2)}) async-start(bf16[8,128,1792]{2,1,0:T(8,128)(2,1)} %shard_map.240), calls=%async_computation.2 | async-start | bytes 7340032 | tf_op jit(solution)/shard_map/all_to_all | solution.py:180
  200.9 2.9 collective-permute-start.31
  206.2 8.3 %collective-permute-start.37 = (bf16[128,1024]{1,0:T(8,128)(2,1)S(1)}, bf16[128,1024]{1,0:T(8,128)(2,1)S(1)}, u32[]{:S(2)}, u32[]{:S(2)}) collective-permute-start(bf16[128,1024]{1,0:T(8,128)(2,1)S(1)} %collective-permute-done.36.refs_14_), channel_id=1, source_target_pairs={{0,8},{8,0},{16,24},{24,16},{32,40},{40,32},{48,56},{56,48},{1,9},... | collective-permute-start | bytes 786440 | tf_op jit(solution)/shard_map/ppermute | solution.py:90
  214.5 3.4 collective-permute-start.35
  218.0 23.9 %all-to-all-done.2.parts = bf16[8,128,1792]{2,1,0:T(8,128)(2,1)} async-done(((bf16[8,128,1792]{2,1,0:T(8,128)(2,1)}), bf16[8,128,1792]{2,1,0:T(8,128)(2,1)}, u32[]{:S(2)}, u32[]{:S(2)}) %all-to-all-start.2) | async-done | bytes 3670048 | tf_op jit(solution)/shard_map/all_to_all | solution.py:180
  241.9 3.2 shard_map.243
  245.5 3.8 %collective-permute-start.40 = (bf16[128,576]{1,0:T(8,128)(2,1)}, bf16[128,576]{1,0:T(8,128)(2,1)S(1)}, u32[]{:S(2)}, u32[]{:S(2)}) collective-permute-start(bf16[128,576]{1,0:T(8,128)(2,1)} %get-tuple-element.184), channel_id=1, source_target_pairs={{0,64},{1,72},{2,80},{3,88},{4,96},{5,104},{6,112},{7,120},{8,65},... | collective-permute-start | bytes 442376 | tf_op jit(solution)/shard_map/ppermute | solution.py:134
  249.4 2.7 collective-permute-start.39
  252.2 5.3 %shard_map.244 = bf16[8,128,512]{2,1,0:T(8,128)(2,1)} custom-call(bf16[128,1024]{1,0:T(8,128)(2,1)} %copy-done.12, bf16[128,1024]{1,0:T(8,128)(2,1)} %copy-done.28, bf16[128,1024]{1,0:T(8,128)(2,1)} %copy-done.27, bf16[128,1024]{1,0:T(8,128)(2,1)} %copy-done.29, bf16[128,1024]{1,0:T(8,128)(2,1)} %copy-done.26, bf16[128,1024]{1,0:T(8,128)(2,1)} %copy-done.30, ...), custom_call_target="tpu_custom_call" | custom-call | flops 1000000000 | bytes 6562304 | tf_op jit(solution)/shard_map/pallas_call | solution.py:35
  261.1 14.8 %all-to-all-start.3 = ((bf16[8,128,512]{2,1,0:T(8,128)(2,1)}), bf16[8,128,512]{2,1,0:T(8,128)(2,1)S(1)}, u32[]{:S(2)}, u32[]{:S(2)}) async-start(bf16[8,128,512]{2,1,0:T(8,128)(2,1)} %shard_map.244), calls=%async_computation.3 | async-start | bytes 2097152 | tf_op jit(solution)/shard_map/all_to_all | solution.py:180
  282.4 10.7 %all-to-all-done.3.parts = bf16[8,128,512]{2,1,0:T(8,128)(2,1)S(1)} async-done(((bf16[8,128,512]{2,1,0:T(8,128)(2,1)}), bf16[8,128,512]{2,1,0:T(8,128)(2,1)S(1)}, u32[]{:S(2)}, u32[]{:S(2)}) %all-to-all-start.3) | async-done | bytes 1048608 | tf_op jit(solution)/shard_map/all_to_all | solution.py:180
  297.4 3.4 collective-permute-done.43.out_other
  303.4 4.3 %collective-permute-done.42.out = bf16[128,128]{1,0:T(8,128)(2,1)S(1)} collective-permute-done((bf16[128,128]{1,0:T(8,128)(2,1)}, bf16[128,128]{1,0:T(8,128)(2,1)S(1)}, u32[]{:S(2)}, u32[]{:S(2)}) %collective-permute-start.42) | collective-permute-done | bytes 32800 | tf_op jit(solution)/shard_map/ppermute | solution.py:134
  311.8 7.9 %collective-permute-start.49 = (bf16[128,512]{1,0:T(8,128)(2,1)}, bf16[128,512]{1,0:T(8,128)(2,1)S(1)}, u32[]{:S(2)}, u32[]{:S(2)}) collective-permute-start(bf16[128,512]{1,0:T(8,128)(2,1)} %shard_map.247.refs_1_), channel_id=1, source_target_pairs={{0,32},{8,40},{16,48},{24,56},{32,0},{40,8},{48,16},{56,24},{1,33}... | collective-permute-start | bytes 393224 | tf_op jit(solution)/shard_map/ppermute | solution.py:94
  322.8 6.4 %shard_map.248 = (f32[128,4608]{1,0:T(8,128)}, f32[128,4608]{1,0:T(8,128)}, f32[576,1024]{1,0:T(8,128)}) custom-call(s32[8]{0:T(128)} %stack.95.order.refs_0_, bf16[128,1728]{1,0:T(8,128)(2,1)} %shard_map.245.refs_1_, bf16[128,1728]{1,0:T(8,128)(2,1)} %copy-done.20, bf16[128,1728]{1,0:T(8,128)(2,1)} %collective-permute-done.44.refs_3_, ...), custom_call_target="tpu_custom_call" | custom-call | flops 1000000 | bytes 10616864 | tf_op jit(solution)/shard_map/pallas_call | solution.py:35
  333.2 3.3 shard_map.249
  (305 shorter events, 102.2 us)
Async XLA Ops:
  7.2 119.2 %all-gather.2.cloned.1.call-start = ((), (), s32[]{:S(2)}) async-start(), calls=%async_computation.6 | async-start | bytes 4128768 | tf_op jit(solution)/shard_map/all_gather | solution.py:526
  19.0 20.5 %collective-permute-start.2 = (bf16[128,1024]{1,0:T(8,128)(2,1)S(1)}, bf16[128,1024]{1,0:T(8,128)(2,1)S(1)}, u32[]{:S(2)}, u32[]{:S(2)}) collective-permute-start(bf16[128,1024]{1,0:T(8,128)(2,1)S(1)} %fusion.3.refs_0_), channel_id=1, source_target_pairs={{0,32},{8,40},{16,48},{24,56},{32,0},{40,8},{48,16},{56,24},{1,33}... | collective-permute-start | bytes 786440 | tf_op jit(solution)/shard_map/ppermute | solution.py:94
  29.2 11.3 %collective-permute-start = (bf16[128,1024]{1,0:T(8,128)(2,1)S(1)}, bf16[128,1024]{1,0:T(8,128)(2,1)S(1)}, u32[]{:S(2)}, u32[]{:S(2)}) collective-permute-start(bf16[128,1024]{1,0:T(8,128)(2,1)S(1)} %fusion.3.refs_0_), channel_id=1, source_target_pairs={{0,16},{8,24},{16,32},{24,40},{32,48},{40,56},{48,0},{56,8},{1,17}... | collective-permute-start | bytes 786440 | tf_op jit(solution)/shard_map/ppermute | solution.py:94
  30.6 33.0 %collective-permute-start.7 = (bf16[128,1024]{1,0:T(8,128)(2,1)}, bf16[128,1024]{1,0:T(8,128)(2,1)}, u32[]{:S(2)}, u32[]{:S(2)}) collective-permute-start(bf16[128,1024]{1,0:T(8,128)(2,1)} %param.23), channel_id=1, source_target_pairs={{0,1},{1,0},{2,3},{3,2},{4,5},{5,4},{6,7},{7,6},{8,9},{9,8},{10,11... | collective-permute-start | bytes 786440 | tf_op jit(solution)/shard_map/ppermute | solution.py:143
  35.1 15.9 %all-to-all-start = ((bf16[8,128,256]{2,1,0:T(8,128)(2,1)}), bf16[8,128,256]{2,1,0:T(8,128)(2,1)S(1)}, u32[]{:S(2)}, u32[]{:S(2)}) async-start(bf16[8,128,256]{2,1,0:T(8,128)(2,1)} %broadcast_in_dim.20), calls=%async_computation | async-start | bytes 1048576 | tf_op jit(solution)/shard_map/all_to_all | solution.py:180
  52.6 50.7 %all-to-all-start.1 = ((bf16[8,128,1024]{2,1,0:T(8,128)(2,1)}), bf16[8,128,1024]{2,1,0:T(8,128)(2,1)S(1)}, u32[]{:S(2)}, u32[]{:S(2)}) async-start(bf16[8,128,1024]{2,1,0:T(8,128)(2,1)} %broadcast_in_dim.22), calls=%async_computation.1 | async-start | bytes 4194304 | tf_op jit(solution)/shard_map/all_to_all | solution.py:180
  58.8 218.8 %reduce-scatter.5.cloned.1.call-start = ((), (), s32[]{:S(2)}) async-start(), calls=%async_computation.8 | async-start | bytes 2359296 | tf_op jit(solution)/shard_map/reduce_scatter | solution.py:585
  66.7 25.9 %collective-permute-start.14 = (bf16[256,1024]{1,0:T(8,128)(2,1)S(1)}, bf16[256,1024]{1,0:T(8,128)(2,1)S(1)}, u32[]{:S(2)}, u32[]{:S(2)}) collective-permute-start(bf16[256,1024]{1,0:T(8,128)(2,1)S(1)} %pad_maximum_fusion.refs_0_), channel_id=1, source_target_pairs={{0,4},{1,5},{2,6},{3,7},{4,0},{5,1},{6,2},{7,3},{8,12},{9,13},{10,... | collective-permute-start | bytes 1572872 | tf_op jit(solution)/shard_map/ppermute | solution.py:143
  67.2 34.9 %collective-permute-start.13 = (bf16[256,1024]{1,0:T(8,128)(2,1)S(1)}, bf16[256,1024]{1,0:T(8,128)(2,1)S(1)}, u32[]{:S(2)}, u32[]{:S(2)}) collective-permute-start(bf16[256,1024]{1,0:T(8,128)(2,1)S(1)} %pad_maximum_fusion.refs_0_), channel_id=1, source_target_pairs={{0,6},{1,7},{2,0},{3,1},{4,2},{5,3},{6,4},{7,5},{8,14},{9,15},{10,... | collective-permute-start | bytes 1572872 | tf_op jit(solution)/shard_map/ppermute | solution.py:143
  68.4 34.9 %collective-permute-start.12 = (bf16[256,1024]{1,0:T(8,128)(2,1)S(1)}, bf16[256,1024]{1,0:T(8,128)(2,1)}, u32[]{:S(2)}, u32[]{:S(2)}) collective-permute-start(bf16[256,1024]{1,0:T(8,128)(2,1)S(1)} %pad_maximum_fusion.refs_0_), channel_id=1, source_target_pairs={{0,2},{1,3},{2,4},{3,5},{4,6},{5,7},{6,0},{7,1},{8,10},{9,11},{10,... | collective-permute-start | bytes 1572872 | tf_op jit(solution)/shard_map/ppermute | solution.py:143
  110.8 12.1 %collective-permute-start.18 = (bf16[128,1024]{1,0:T(8,128)(2,1)}, bf16[128,1024]{1,0:T(8,128)(2,1)S(1)}, u32[]{:S(2)}, u32[]{:S(2)}) collective-permute-start(bf16[128,1024]{1,0:T(8,128)(2,1)} %get-tuple-element.144.refs_1_), channel_id=1, source_target_pairs={{0,48},{8,56},{16,0},{24,8},{32,16},{40,24},{48,32},{56,40},{1,49}... | collective-permute-start | bytes 786440 | tf_op jit(solution)/shard_map/ppermute | solution.py:94
  111.6 12.7 %collective-permute-start.16 = (bf16[128,1024]{1,0:T(8,128)(2,1)}, bf16[128,1024]{1,0:T(8,128)(2,1)S(1)}, u32[]{:S(2)}, u32[]{:S(2)}) collective-permute-start(bf16[128,1024]{1,0:T(8,128)(2,1)} %get-tuple-element.144.refs_1_), channel_id=1, source_target_pairs={{0,16},{8,24},{16,32},{24,40},{32,48},{40,56},{48,0},{56,8},{1,17}... | collective-permute-start | bytes 786440 | tf_op jit(solution)/shard_map/ppermute | solution.py:94
  112.3 12.6 %collective-permute-start.15 = (bf16[128,1024]{1,0:T(8,128)(2,1)}, bf16[128,1024]{1,0:T(8,128)(2,1)S(1)}, u32[]{:S(2)}, u32[]{:S(2)}) collective-permute-start(bf16[128,1024]{1,0:T(8,128)(2,1)} %get-tuple-element.144.refs_1_), channel_id=1, source_target_pairs={{0,8},{8,0},{16,24},{24,16},{32,40},{40,32},{48,56},{56,48},{1,9},... | collective-permute-start | bytes 786440 | tf_op jit(solution)/shard_map/ppermute | solution.py:90
  141.8 137.5 %reduce-scatter.3.cloned.1.call-start = ((), (), s32[]{:S(2)}) async-start(), calls=%async_computation.7 | async-start | bytes 2359296 | tf_op jit(solution)/shard_map/reduce_scatter | solution.py:622
  146.0 13.3 %collective-permute-start.26 = (bf16[128,1024]{1,0:T(8,128)(2,1)S(1)}, bf16[128,1024]{1,0:T(8,128)(2,1)S(1)}, u32[]{:S(2)}, u32[]{:S(2)}) collective-permute-start(bf16[128,1024]{1,0:T(8,128)(2,1)S(1)} %get-tuple-element.215), channel_id=1, source_target_pairs={{0,16},{8,24},{16,32},{24,40},{32,48},{40,56},{48,0},{56,8},{1,17}... | collective-permute-start | bytes 786440 | tf_op jit(solution)/shard_map/ppermute | solution.py:94
  146.9 12.4 %collective-permute-start.25 = (bf16[128,1024]{1,0:T(8,128)(2,1)S(1)}, bf16[128,1024]{1,0:T(8,128)(2,1)S(1)}, u32[]{:S(2)}, u32[]{:S(2)}) collective-permute-start(bf16[128,1024]{1,0:T(8,128)(2,1)S(1)} %get-tuple-element.216), channel_id=1, source_target_pairs={{0,48},{8,56},{16,0},{24,8},{32,16},{40,24},{48,32},{56,40},{1,49}... | collective-permute-start | bytes 786440 | tf_op jit(solution)/shard_map/ppermute | solution.py:94
  148.6 16.5 %collective-permute-start.24 = (bf16[128,1024]{1,0:T(8,128)(2,1)S(1)}, bf16[128,1024]{1,0:T(8,128)(2,1)S(1)}, u32[]{:S(2)}, u32[]{:S(2)}) collective-permute-start(bf16[128,1024]{1,0:T(8,128)(2,1)S(1)} %get-tuple-element.217), channel_id=1, source_target_pairs={{0,32},{8,40},{16,48},{24,56},{32,0},{40,8},{48,16},{56,24},{1,33}... | collective-permute-start | bytes 786440 | tf_op jit(solution)/shard_map/ppermute | solution.py:94
  193.3 48.6 %all-to-all-start.2 = ((bf16[8,128,1792]{2,1,0:T(8,128)(2,1)}), bf16[8,128,1792]{2,1,0:T(8,128)(2,1)}, u32[]{:S(2)}, u32[]{:S(2)}) async-start(bf16[8,128,1792]{2,1,0:T(8,128)(2,1)} %shard_map.240), calls=%async_computation.2 | async-start | bytes 7340032 | tf_op jit(solution)/shard_map/all_to_all | solution.py:180
  198.9 15.6 %collective-permute-start.34 = (bf16[128,1024]{1,0:T(8,128)(2,1)S(1)}, bf16[128,1024]{1,0:T(8,128)(2,1)S(1)}, u32[]{:S(2)}, u32[]{:S(2)}) collective-permute-start(bf16[128,1024]{1,0:T(8,128)(2,1)S(1)} %copy-done.32), channel_id=1, source_target_pairs={{0,48},{8,56},{16,0},{24,8},{32,16},{40,24},{48,32},{56,40},{1,49}... | collective-permute-start | bytes 786440 | tf_op jit(solution)/shard_map/ppermute | solution.py:94
  200.9 17.0 %collective-permute-start.32 = (bf16[128,1024]{1,0:T(8,128)(2,1)S(1)}, bf16[128,1024]{1,0:T(8,128)(2,1)S(1)}, u32[]{:S(2)}, u32[]{:S(2)}) collective-permute-start(bf16[128,1024]{1,0:T(8,128)(2,1)S(1)} %copy-done.32), channel_id=1, source_target_pairs={{0,16},{8,24},{16,32},{24,40},{32,48},{40,56},{48,0},{56,8},{1,17}... | collective-permute-start | bytes 786440 | tf_op jit(solution)/shard_map/ppermute | solution.py:94
  200.9 44.1 %collective-permute-start.31 = (bf16[128,1024]{1,0:T(8,128)(2,1)S(1)}, bf16[128,1024]{1,0:T(8,128)(2,1)S(1)}, u32[]{:S(2)}, u32[]{:S(2)}) collective-permute-start(bf16[128,1024]{1,0:T(8,128)(2,1)S(1)} %copy-done.32), channel_id=1, source_target_pairs={{0,8},{8,0},{16,24},{24,16},{32,40},{40,32},{48,56},{56,48},{1,9},... | collective-permute-start | bytes 786440 | tf_op jit(solution)/shard_map/ppermute | solution.py:90
  206.2 38.9 %collective-permute-start.37 = (bf16[128,1024]{1,0:T(8,128)(2,1)S(1)}, bf16[128,1024]{1,0:T(8,128)(2,1)S(1)}, u32[]{:S(2)}, u32[]{:S(2)}) collective-permute-start(bf16[128,1024]{1,0:T(8,128)(2,1)S(1)} %collective-permute-done.36.refs_14_), channel_id=1, source_target_pairs={{0,8},{8,0},{16,24},{24,16},{32,40},{40,32},{48,56},{56,48},{1,9},... | collective-permute-start | bytes 786440 | tf_op jit(solution)/shard_map/ppermute | solution.py:90
  214.5 30.6 %collective-permute-start.35 = (bf16[128,1024]{1,0:T(8,128)(2,1)S(1)}, bf16[128,1024]{1,0:T(8,128)(2,1)S(1)}, u32[]{:S(2)}, u32[]{:S(2)}) collective-permute-start(bf16[128,1024]{1,0:T(8,128)(2,1)S(1)} %collective-permute-done.34.refs_12_), channel_id=1, source_target_pairs={{0,8},{8,0},{16,24},{24,16},{32,40},{40,32},{48,56},{56,48},{1,9},... | collective-permute-start | bytes 786440 | tf_op jit(solution)/shard_map/ppermute | solution.py:90
  217.9 27.2 %collective-permute-start.33 = (bf16[128,1024]{1,0:T(8,128)(2,1)S(1)}, bf16[128,1024]{1,0:T(8,128)(2,1)S(1)}, u32[]{:S(2)}, u32[]{:S(2)}) collective-permute-start(bf16[128,1024]{1,0:T(8,128)(2,1)S(1)} %collective-permute-done.32.refs_10_), channel_id=1, source_target_pairs={{0,8},{8,0},{16,24},{24,16},{32,40},{40,32},{48,56},{56,48},{1,9},... | collective-permute-start | bytes 786440 | tf_op jit(solution)/shard_map/ppermute | solution.py:90
  245.1 12.6 %collective-permute-start.38 = (bf16[128,1152]{1,0:T(8,128)(2,1)}, bf16[128,1152]{1,0:T(8,128)(2,1)S(1)}, u32[]{:S(2)}, u32[]{:S(2)}) collective-permute-start(bf16[128,1152]{1,0:T(8,128)(2,1)} %get-tuple-element.183.own), channel_id=1, source_target_pairs={{0,64},{64,0},{1,65},{65,1},{2,66},{66,2},{3,67},{67,3},{4,68},{68... | collective-permute-start | bytes 884744 | tf_op jit(solution)/shard_map/ppermute | solution.py:138
  245.5 12.0 %collective-permute-start.40 = (bf16[128,576]{1,0:T(8,128)(2,1)}, bf16[128,576]{1,0:T(8,128)(2,1)S(1)}, u32[]{:S(2)}, u32[]{:S(2)}) collective-permute-start(bf16[128,576]{1,0:T(8,128)(2,1)} %get-tuple-element.184), channel_id=1, source_target_pairs={{0,64},{1,72},{2,80},{3,88},{4,96},{5,104},{6,112},{7,120},{8,65},... | collective-permute-start | bytes 442376 | tf_op jit(solution)/shard_map/ppermute | solution.py:134
  261.1 32.0 %all-to-all-start.3 = ((bf16[8,128,512]{2,1,0:T(8,128)(2,1)}), bf16[8,128,512]{2,1,0:T(8,128)(2,1)S(1)}, u32[]{:S(2)}, u32[]{:S(2)}) async-start(bf16[8,128,512]{2,1,0:T(8,128)(2,1)} %shard_map.244), calls=%async_computation.3 | async-start | bytes 2097152 | tf_op jit(solution)/shard_map/all_to_all | solution.py:180
  276.0 34.7 %collective-permute-start.46 = (bf16[128,1728]{1,0:T(8,128)(2,1)S(1)}, bf16[128,1728]{1,0:T(8,128)(2,1)}, u32[]{:S(2)}, u32[]{:S(2)}) collective-permute-start(bf16[128,1728]{1,0:T(8,128)(2,1)S(1)} %copy-done.11), channel_id=1, source_target_pairs={{0,32},{8,40},{16,48},{24,56},{32,0},{40,8},{48,16},{56,24},{1,33}... | collective-permute-start | bytes 1327112 | tf_op jit(solution)/shard_map/ppermute | solution.py:94
  276.1 34.7 %collective-permute-start.45 = (bf16[128,1728]{1,0:T(8,128)(2,1)S(1)}, bf16[128,1728]{1,0:T(8,128)(2,1)}, u32[]{:S(2)}, u32[]{:S(2)}) collective-permute-start(bf16[128,1728]{1,0:T(8,128)(2,1)S(1)} %copy-done.11), channel_id=1, source_target_pairs={{0,48},{8,56},{16,0},{24,8},{32,16},{40,24},{48,32},{56,40},{1,49}... | collective-permute-start | bytes 1327112 | tf_op jit(solution)/shard_map/ppermute | solution.py:94
  277.4 33.4 %collective-permute-start.44 = (bf16[128,1728]{1,0:T(8,128)(2,1)S(1)}, bf16[128,1728]{1,0:T(8,128)(2,1)}, u32[]{:S(2)}, u32[]{:S(2)}) collective-permute-start(bf16[128,1728]{1,0:T(8,128)(2,1)S(1)} %copy-done.11), channel_id=1, source_target_pairs={{0,16},{8,24},{16,32},{24,40},{32,48},{40,56},{48,0},{56,8},{1,17}... | collective-permute-start | bytes 1327112 | tf_op jit(solution)/shard_map/ppermute | solution.py:94
  296.0 11.7 %collective-permute-start.41 = (bf16[128,384]{1,0:T(8,128)(2,1)}, bf16[128,384]{1,0:T(8,128)(2,1)S(1)}, u32[]{:S(2)}, u32[]{:S(2)}) collective-permute-start(bf16[128,384]{1,0:T(8,128)(2,1)} %get-tuple-element.192.own), channel_id=1, source_target_pairs={{0,64},{64,0},{1,65},{65,1},{2,66},{66,2},{3,67},{67,3},{4,68},{68... | collective-permute-start | bytes 294920 | tf_op jit(solution)/shard_map/ppermute | solution.py:138
  311.8 17.4 %collective-permute-start.49 = (bf16[128,512]{1,0:T(8,128)(2,1)}, bf16[128,512]{1,0:T(8,128)(2,1)S(1)}, u32[]{:S(2)}, u32[]{:S(2)}) collective-permute-start(bf16[128,512]{1,0:T(8,128)(2,1)} %shard_map.247.refs_1_), channel_id=1, source_target_pairs={{0,32},{8,40},{16,48},{24,56},{32,0},{40,8},{48,16},{56,24},{1,33}... | collective-permute-start | bytes 393224 | tf_op jit(solution)/shard_map/ppermute | solution.py:94
  (106 other events, 868.7 us)
Sparse Core Ops, SparseCore 0:
  18.8 82.6 all-gather.1
  141.9 36.2 reduce-scatter.4
  193.4 38.7 reduce-scatter.2

commit v3 on v0

--- a/solution.py
+++ b/solution.py
@@ -99,6 +99,13 @@
     for step in STEPS:
         mine = block if step == 0 else move_z(block, -step)
         pieces += [mine, swap_core(mine)]
+    return pieces
+
+
+def swap_pieces(moved):
+    pieces = []
+    for piece in moved:
+        pieces += [piece, swap_core(piece)]
     return pieces
 
 
@@ -503,7 +510,7 @@
     first_scale = rms_scale(tokens)
     first_hat = tokens * first_scale
     first_normed = (first_hat * attn_gain).astype(BF16)
-    first_pieces = gather_ctx(first_normed)
+    first_moved = [move_z(first_normed, -step) if step else first_normed for step in STEPS]
     qkv_block = jnp.concatenate(
         [own_columns(w_query, q_width, ctx), own_columns(w_key, k_width, ctx), own_columns(w_value, k_width, ctx)],
         axis=1,
@@ -518,9 +525,11 @@
     )
     ffn_block, w_qkv = stage(ffn_block, w_qkv)
     ffn_rows = lax.all_gather(ffn_block, "fsdp", axis=0, tiled=True)
-    first_pieces, w_qkv, tables, out_pair, cot_copies = stage(first_pieces, w_qkv, tables, out_pair, cot_copies)
-
+    w_qkv, first_moved, cot_copies = stage(w_qkv, first_moved, cot_copies)
     cots = all_to_all(cot_copies, "ctx")
+    first_pieces = swap_pieces(first_moved)
+    first_pieces, w_qkv, tables, out_pair = stage(first_pieces, w_qkv, tables, out_pair)
+
     out_pairs = spread_y(out_pair)
     qkv, lse, own, other = call(
         attend_forward,
@@ -534,7 +543,7 @@
     )
 
     mixed_blocks = exchange_ctx(own, other)
-    mixed_blocks, out_pairs = stage(mixed_blocks, out_pairs)
+    mixed_blocks, out_pairs, cots = stage(mixed_blocks, out_pairs, cots)
     square = pltpu.VMEM((width, width), BF16)
     residual, second_normed = call(
         out_project,

time: 334 us -> 341 us (1.021)
  starting transfers between devices: 115 us -> 120 us
  waiting for transfers between devices: 82.5 us -> 87.3 us
    ppermute x4, waiting for transfers between devices: 1.63 us -> 10.4 us  [move_y(): return lax.ppermute(value, 'fsdp', pairs)]
    ppermute x24, waiting for transfers between devices: 49.4 us -> 43.6 us  [move_z(): lax.ppermute(value, 'ctx', [(i, (i + 2 * step) % 8) for i in range(8)])]
    unnamed x135 -> x141, local copies, waits for them, and re-layouts: 9.31 us -> 7.1 us
  transfers between devices with their start and end apart: 65 -> 65, of which waited for: 23 -> 33; matrix products, arithmetic and copies ran while one was open for 6% -> 6% of each run, Pallas kernels for 20% -> 20%
where the time goes in v3:
time: 341 us; the launch traced here: 334 us
  starting transfers between devices  120 us (35%)
  waiting for transfers between devices  87.3 us (26%)
  Pallas kernels  81.3 us (24%)
  local copies, waits for them, and re-layouts  21.5 us (6%)
  between operations  14.8 us (4%)
  other arithmetic  9.64 us (3%)
    pallas_call x13, Pallas kernels, call(): pl.pallas_call(kernel, out_shape=out_shapes, in_specs=[pl.BlockSpec(memor...  81.3 us
    ppermute x24, waiting for transfers between devices, move_z(): lax.ppermute(value, 'ctx', [(i, (i + 2 * step) % 8) for i in range(8)])  43.6 us
    ppermute x23, starting transfers between devices, swap_core(): return lax.ppermute(value, 'ctx', [(i, i ^ 1) for i in range(8)])  38.7 us
    all_to_all x4, starting transfers between devices, all_to_all(): return lax.all_to_all(blocks, axis, split_axis=0, concat_axis=0, tiled=True)  27.6 us
    ppermute x24, starting transfers between devices, move_z(): lax.ppermute(value, 'ctx', [(i, (i + 2 * step) % 8) for i in range(8)])  27.1 us
    ppermute x5, waiting for transfers between devices, transpose_mesh(): return lax.ppermute(value, ('dp', 'ctx', 'fsdp'), pairs)  26.8 us
    ppermute x5, starting transfers between devices, transpose_mesh(): return lax.ppermute(value, ('dp', 'ctx', 'fsdp'), pairs)  19.7 us
    ppermute x4, waiting for transfers between devices, move_y(): return lax.ppermute(value, 'fsdp', pairs)  10.4 us
  transfers between devices with their start and end apart: 65, of which 33 were waited for; matrix products, arithmetic and copies ran while one was open for 6% of the time, Pallas kernels for 20%

profile of v3, /device:TPU:31, one launch (start us, length us, event | category | flops | bytes accessed | tf_op | source)
XLA Modules:
  0.0 334.5 jit_solution(1041677767537526735)
XLA Ops:
  9.9 6.7 %all-to-all-start = ((bf16[8,128,256]{2,1,0:T(8,128)(2,1)}), bf16[8,128,256]{2,1,0:T(8,128)(2,1)S(1)}, u32[]{:S(2)}, u32[]{:S(2)}) async-start(bf16[8,128,256]{2,1,0:T(8,128)(2,1)} %broadcast_in_dim.20), calls=%async_computation | async-start | bytes 1048576 | tf_op jit(solution)/shard_map/all_to_all | solution.py:180
  16.8 5.7 %collective-permute-start = (bf16[128,576]{1,0:T(8,128)(2,1)S(1)}, bf16[128,576]{1,0:T(8,128)(2,1)S(1)}, u32[]{:S(2)}, u32[]{:S(2)}) collective-permute-start(bf16[128,576]{1,0:T(8,128)(2,1)S(1)} %bitcast.79), channel_id=1, source_target_pairs={{0,0},{1,8},{2,16},{3,24},{4,32},{5,40},{6,48},{7,56},{8,1},{9,9},... | collective-permute-start | bytes 442376 | tf_op jit(solution)/shard_map/ppermute | solution.py:134
  23.7 10.2 %collective-permute-done = bf16[128,576]{1,0:T(8,128)(2,1)S(1)} collective-permute-done((bf16[128,576]{1,0:T(8,128)(2,1)S(1)}, bf16[128,576]{1,0:T(8,128)(2,1)S(1)}, u32[]{:S(2)}, u32[]{:S(2)}) %collective-permute-start) | collective-permute-done | bytes 147488 | tf_op jit(solution)/shard_map/ppermute | solution.py:134
  39.6 5.5 %collective-permute-done.3.refs_6_ = bf16[128,1024]{1,0:T(8,128)(2,1)S(1)} collective-permute-done((bf16[128,1024]{1,0:T(8,128)(2,1)S(1)}, bf16[128,1024]{1,0:T(8,128)(2,1)S(1)}, u32[]{:S(2)}, u32[]{:S(2)}) %collective-permute-start.3) | collective-permute-done | bytes 262176 | tf_op jit(solution)/shard_map/ppermute | solution.py:94
  45.1 2.9 collective-permute-done.2.refs_4_
  50.2 5.5 %all-to-all-start.1 = ((bf16[8,128,1024]{2,1,0:T(8,128)(2,1)}), bf16[8,128,1024]{2,1,0:T(8,128)(2,1)}, u32[]{:S(2)}, u32[]{:S(2)}) async-start(bf16[8,128,1024]{2,1,0:T(8,128)(2,1)} %broadcast_in_dim.22), calls=%async_computation.1 | async-start | bytes 4194304 | tf_op jit(solution)/shard_map/all_to_all | solution.py:180
  68.1 12.2 %shard_map.237 = (f32[256,1024]{1,0:T(8,128)}, f32[8,1024]{1,0:T(8,128)}, bf16[4,128,128]{2,1,0:T(8,128)(2,1)}, bf16[4,128,128]{2,1,0:T(8,128)(2,1)}) custom-call(bf16[128,1024]{1,0:T(8,128)(2,1)} %copy-done.11, bf16[128,1024]{1,0:T(8,128)(2,1)} %copy-done.25, bf16[128,1024]{1,0:T(8,128)(2,1)} %copy-done.24, bf16[128,1024]{1,0:T(8,128)(2,1)} %copy-done.26, ...), custom_call_target="tpu_custom_call" | custom-call | flops 4000000000 | bytes 5280256 | tf_op jit(solution)/shard_map/pallas_call | solution.py:35
  91.8 10.1 %collective-permute-done.14.refs_2_ = bf16[256,1024]{1,0:T(8,128)(2,1)S(1)} collective-permute-done((bf16[256,1024]{1,0:T(8,128)(2,1)S(1)}, bf16[256,1024]{1,0:T(8,128)(2,1)S(1)}, u32[]{:S(2)}, u32[]{:S(2)}) %collective-permute-start.14) | collective-permute-done | bytes 524320 | tf_op jit(solution)/shard_map/ppermute | solution.py:143
  103.0 4.1 %shard_map.238 = (f32[128,1024]{1,0:T(8,128)}, bf16[128,1024]{1,0:T(8,128)(2,1)}) custom-call(s32[2]{0:T(128)} %pad_add_fusion.place, s32[8]{0:T(128)} %stack.89.order.refs_0_, bf16[256,1024]{1,0:T(8,128)(2,1)} %copy-done.4, bf16[256,1024]{1,0:T(8,128)(2,1)} %copy-done.9, bf16[256,1024]{1,0:T(8,128)(2,1)} %copy-done.8, bf16[256,1024]{1,0:T(8,128)(2,1)} %copy-done.7, ...), custom_call_target="tpu_custom_call" | custom-call | flops 300000000 | bytes 3412008 | tf_op jit(solution)/shard_map/pallas_call | solution.py:35
  111.3 2.8 collective-permute-start.16
  114.9 4.9 %collective-permute-start.22 = (bf16[128,1024]{1,0:T(8,128)(2,1)S(1)}, bf16[128,1024]{1,0:T(8,128)(2,1)S(1)}, u32[]{:S(2)}, u32[]{:S(2)}) collective-permute-start(bf16[128,1024]{1,0:T(8,128)(2,1)S(1)} %collective-permute-done.21.refs_7_), channel_id=1, source_target_pairs={{0,8},{8,0},{16,24},{24,16},{32,40},{40,32},{48,56},{56,48},{1,9},... | collective-permute-start | bytes 786440 | tf_op jit(solution)/shard_map/ppermute | solution.py:90
  125.9 15.3 %shard_map.239 = (bf16[1024,576]{1,0:T(8,128)(2,1)}, bf16[1024,1152]{1,0:T(8,128)(2,1)}, bf16[8,128,1024]{2,1,0:T(8,128)(2,1)}, bf16[4,128,1024]{2,1,0:T(8,128)(...) custom-call(s32[8]{0:T(128)} %stack.89.order.refs_0_, ...), custom_call_target="tpu_custom_call" | custom-call | flops 8000000000 | bytes 16515104 | tf_op jit(solution)/shard_map/pallas_call | solution.py:35
  149.1 9.7 %shard_map.240 = bf16[8,128,1792]{2,1,0:T(8,128)(2,1)} custom-call(s32[8]{0:T(128)} %stack.89.order.refs_0_, bf16[128,1024]{1,0:T(8,128)(2,1)} %get-tuple-element.136.refs_1_, bf16[128,1024]{1,0:T(8,128)(2,1)} %copy-done.63, bf16[128,1024]{1,0:T(8,128)(2,1)} %copy-done.62, bf16[128,1024]{1,0:T(8,128)(2,1)} %copy-done.66, bf16[128,1024]{1,0:T(8,128)(2,1)} %copy-done.61, ...), custom_call_target="tpu_custom_call" | custom-call | flops 4000000000 | bytes 11403296 | tf_op jit(solution)/shard_map/pallas_call | solution.py:35
  158.8 9.1 %all-to-all-start.2 = ((bf16[8,128,1792]{2,1,0:T(8,128)(2,1)}), bf16[8,128,1792]{2,1,0:T(8,128)(2,1)}, u32[]{:S(2)}, u32[]{:S(2)}) async-start(bf16[8,128,1792]{2,1,0:T(8,128)(2,1)} %shard_map.240), calls=%async_computation.4 | async-start | bytes 7340032 | tf_op jit(solution)/shard_map/all_to_all | solution.py:180
  168.8 4.7 %shard_map.241 = (f32[128,1024]{1,0:T(8,128)}, bf16[128,1024]{1,0:T(8,128)(2,1)}, f32[1,1024]{1,0:T(1,128)}, bf16[4,128,128]{2,1,0:T(8,128)(2,1)}, bf16[4,128,128]{2,1,0:T(8,128)(2,1)}) custom-call(s32[2]{0:T(128)} %pad_add_fusion.place, s32[8]{0:T(128)} %stack.89.order.refs_0_, bf16[256,1024]{1,0:T(8,128)(2,1)} %copy-done.4, bf16[256,1024]{1,0:T(8,128)(2,1)} %copy-done.9, ...), custom_call_target="tpu_custom_call" | custom-call | flops 300000000 | bytes 5251112 | tf_op jit(solution)/shard_map/pallas_call | solution.py:35
  185.0 11.6 %shard_map.242 = (f32[64,1]{1,0:T(8,128)}, f32[64,1]{1,0:T(8,128)}, bf16[1024,256]{1,0:T(8,128)(2,1)}, bf16[8,128,1024]{2,1,0:T(8,128)(2,1)}) custom-call(s32[8]{0:T(128)} %stack.89.order.refs_0_, bf16[1024,256]{1,0:T(8,128)(2,1)} %bitcast.74, bf16[2,128,128]{2,1,0:T(8,128)(2,1)} %pad_maximum_fusion.6.refs_2_, bf16[2,128,128]{2,1,0:T(8,128)(2,1)} %copy-done.67, ...), custom_call_target="tpu_custom_call" | custom-call | flops 8000000000 | bytes 5805088 | tf_op jit(solution)/shard_map/pallas_call | solution.py:35
  202.0 3.3 collective-permute-done.36.refs_14_
  205.3 4.9 %collective-permute-start.37 = (bf16[128,1024]{1,0:T(8,128)(2,1)S(1)}, bf16[128,1024]{1,0:T(8,128)(2,1)S(1)}, u32[]{:S(2)}, u32[]{:S(2)}) collective-permute-start(bf16[128,1024]{1,0:T(8,128)(2,1)S(1)} %collective-permute-done.36.refs_14_), channel_id=1, source_target_pairs={{0,8},{8,0},{16,24},{24,16},{32,40},{40,32},{48,56},{56,48},{1,9},... | collective-permute-start | bytes 786440 | tf_op jit(solution)/shard_map/ppermute | solution.py:90
  215.3 3.2 shard_map.243
  220.9 5.9 %collective-permute-start.39 = (bf16[128,576]{1,0:T(8,128)(2,1)}, bf16[128,576]{1,0:T(8,128)(2,1)S(1)}, u32[]{:S(2)}, u32[]{:S(2)}) collective-permute-start(bf16[128,576]{1,0:T(8,128)(2,1)} %get-tuple-element.179), channel_id=1, source_target_pairs={{0,0},{1,8},{2,16},{3,24},{4,32},{5,40},{6,48},{7,56},{8,1},{9,9},... | collective-permute-start | bytes 442376 | tf_op jit(solution)/shard_map/ppermute | solution.py:134
  226.8 5.3 %shard_map.244 = bf16[8,128,512]{2,1,0:T(8,128)(2,1)} custom-call(bf16[128,1024]{1,0:T(8,128)(2,1)} %copy-done.11, bf16[128,1024]{1,0:T(8,128)(2,1)} %copy-done.25, bf16[128,1024]{1,0:T(8,128)(2,1)} %copy-done.24, bf16[128,1024]{1,0:T(8,128)(2,1)} %copy-done.26, bf16[128,1024]{1,0:T(8,128)(2,1)} %copy-done.23, bf16[128,1024]{1,0:T(8,128)(2,1)} %copy-done.27, ...), custom_call_target="tpu_custom_call" | custom-call | flops 1000000000 | bytes 6562304 | tf_op jit(solution)/shard_map/pallas_call | solution.py:35
  233.5 7.8 %collective-permute-done.39.down = bf16[128,576]{1,0:T(8,128)(2,1)S(1)} collective-permute-done((bf16[128,576]{1,0:T(8,128)(2,1)}, bf16[128,576]{1,0:T(8,128)(2,1)S(1)}, u32[]{:S(2)}, u32[]{:S(2)}) %collective-permute-start.39) | collective-permute-done | bytes 147488 | tf_op jit(solution)/shard_map/ppermute | solution.py:134
  241.3 6.4 %all-to-all-start.3 = ((bf16[8,128,512]{2,1,0:T(8,128)(2,1)}), bf16[8,128,512]{2,1,0:T(8,128)(2,1)S(1)}, u32[]{:S(2)}, u32[]{:S(2)}) async-start(bf16[8,128,512]{2,1,0:T(8,128)(2,1)} %shard_map.244), calls=%async_computation.5 | async-start | bytes 2097152 | tf_op jit(solution)/shard_map/all_to_all | solution.py:180
  253.2 10.5 %collective-permute-done.56.refs_7_ = bf16[128,1728]{1,0:T(8,128)(2,1)S(1)} collective-permute-done((bf16[128,1728]{1,0:T(8,128)(2,1)}, bf16[128,1728]{1,0:T(8,128)(2,1)S(1)}, u32[]{:S(2)}, u32[]{:S(2)}) %collective-permute-start.56) | collective-permute-done | bytes 442400 | tf_op jit(solution)/shard_map/ppermute | solution.py:94
  263.6 6.9 %collective-permute-done.54.refs_5_ = bf16[128,1728]{1,0:T(8,128)(2,1)S(1)} collective-permute-done((bf16[128,1728]{1,0:T(8,128)(2,1)}, bf16[128,1728]{1,0:T(8,128)(2,1)S(1)}, u32[]{:S(2)}, u32[]{:S(2)}) %collective-permute-start.54) | collective-permute-done | bytes 442400 | tf_op jit(solution)/shard_map/ppermute | solution.py:94
  278.5 3.7 %collective-permute-done.43.out_other = bf16[128,128]{1,0:T(8,128)(2,1)S(1)} collective-permute-done((bf16[128,128]{1,0:T(8,128)(2,1)}, bf16[128,128]{1,0:T(8,128)(2,1)S(1)}, u32[]{:S(2)}, u32[]{:S(2)}) %collective-permute-start.43) | collective-permute-done | bytes 32800 | tf_op jit(solution)/shard_map/ppermute | solution.py:134
  282.2 4.4 %collective-permute-start.42 = (bf16[128,128]{1,0:T(8,128)(2,1)}, bf16[128,128]{1,0:T(8,128)(2,1)S(1)}, u32[]{:S(2)}, u32[]{:S(2)}) collective-permute-start(bf16[128,128]{1,0:T(8,128)(2,1)} %get-tuple-element.182), channel_id=1, source_target_pairs={{0,0},{1,8},{2,16},{3,24},{4,32},{5,40},{6,48},{7,56},{8,1},{9,9},... | collective-permute-start | bytes 98312 | tf_op jit(solution)/shard_map/ppermute | solution.py:134
  286.6 3.8 %collective-permute-done.42.out = bf16[128,128]{1,0:T(8,128)(2,1)S(1)} collective-permute-done((bf16[128,128]{1,0:T(8,128)(2,1)}, bf16[128,128]{1,0:T(8,128)(2,1)S(1)}, u32[]{:S(2)}, u32[]{:S(2)}) %collective-permute-start.42) | collective-permute-done | bytes 32800 | tf_op jit(solution)/shard_map/ppermute | solution.py:134
  290.3 5.1 %collective-permute-start.53 = (bf16[128,1728]{1,0:T(8,128)(2,1)S(1)}, bf16[128,1728]{1,0:T(8,128)(2,1)}, u32[]{:S(2)}, u32[]{:S(2)}) collective-permute-start(bf16[128,1728]{1,0:T(8,128)(2,1)S(1)} %collective-permute-done.52.refs_3_), channel_id=1, source_target_pairs={{0,8},{8,0},{16,24},{24,16},{32,40},{40,32},{48,56},{56,48},{1,9},... | collective-permute-start | bytes 1327112 | tf_op jit(solution)/shard_map/ppermute | solution.py:90
  297.8 4.4 %collective-permute-start.47 = (bf16[128,512]{1,0:T(8,128)(2,1)}, bf16[128,512]{1,0:T(8,128)(2,1)S(1)}, u32[]{:S(2)}, u32[]{:S(2)}) collective-permute-start(bf16[128,512]{1,0:T(8,128)(2,1)} %shard_map.246.refs_1_), channel_id=1, source_target_pairs={{0,48},{8,56},{16,0},{24,8},{32,16},{40,24},{48,32},{56,40},{1,49}... | collective-permute-start | bytes 393224 | tf_op jit(solution)/shard_map/ppermute | solution.py:94
  311.4 6.6 %shard_map.249 = (f32[128,4608]{1,0:T(8,128)}, f32[128,4608]{1,0:T(8,128)}, f32[576,1024]{1,0:T(8,128)}) custom-call(s32[8]{0:T(128)} %stack.89.order.refs_0_, bf16[128,1728]{1,0:T(8,128)(2,1)} %shard_map.248.refs_1_, bf16[128,1728]{1,0:T(8,128)(2,1)} %collective-permute-done.51.refs_2_, bf16[128,1728]{1,0:T(8,128)(2,1)} %copy-done.20, ...), custom_call_target="tpu_custom_call" | custom-call | flops 1000000 | bytes 10616864 | tf_op jit(solution)/shard_map/pallas_call | solution.py:35
  318.8 3.3 shard_map.247
  (299 shorter events, 113.8 us)
Async XLA Ops:
  9.9 25.0 %all-to-all-start = ((bf16[8,128,256]{2,1,0:T(8,128)(2,1)}), bf16[8,128,256]{2,1,0:T(8,128)(2,1)S(1)}, u32[]{:S(2)}, u32[]{:S(2)}) async-start(bf16[8,128,256]{2,1,0:T(8,128)(2,1)} %broadcast_in_dim.20), calls=%async_computation | async-start | bytes 1048576 | tf_op jit(solution)/shard_map/all_to_all | solution.py:180
  16.5 108.7 %all-gather.2.cloned.1.call-start = ((), (), s32[]{:S(2)}) async-start(), calls=%async_computation.6 | async-start | bytes 4128768 | tf_op jit(solution)/shard_map/all_gather | solution.py:527
  16.8 17.1 %collective-permute-start = (bf16[128,576]{1,0:T(8,128)(2,1)S(1)}, bf16[128,576]{1,0:T(8,128)(2,1)S(1)}, u32[]{:S(2)}, u32[]{:S(2)}) collective-permute-start(bf16[128,576]{1,0:T(8,128)(2,1)S(1)} %bitcast.79), channel_id=1, source_target_pairs={{0,0},{1,8},{2,16},{3,24},{4,32},{5,40},{6,48},{7,56},{8,1},{9,9},... | collective-permute-start | bytes 442376 | tf_op jit(solution)/shard_map/ppermute | solution.py:134
  38.2 22.3 %collective-permute-start.8 = (bf16[128,1024]{1,0:T(8,128)(2,1)S(1)}, bf16[128,1024]{1,0:T(8,128)(2,1)S(1)}, u32[]{:S(2)}, u32[]{:S(2)}) collective-permute-start(bf16[128,1024]{1,0:T(8,128)(2,1)S(1)} %copy-done.38), channel_id=1, source_target_pairs={{0,1},{1,0},{2,3},{3,2},{4,5},{5,4},{6,7},{7,6},{8,9},{9,8},{10,11... | collective-permute-start | bytes 786440 | tf_op jit(solution)/shard_map/ppermute | solution.py:143
  50.2 52.0 %all-to-all-start.1 = ((bf16[8,128,1024]{2,1,0:T(8,128)(2,1)}), bf16[8,128,1024]{2,1,0:T(8,128)(2,1)}, u32[]{:S(2)}, u32[]{:S(2)}) async-start(bf16[8,128,1024]{2,1,0:T(8,128)(2,1)} %broadcast_in_dim.22), calls=%async_computation.1 | async-start | bytes 4194304 | tf_op jit(solution)/shard_map/all_to_all | solution.py:180
  55.6 254.0 %reduce-scatter.3.cloned.1.call-start = ((), (), s32[]{:S(2)}) async-start(), calls=%async_computation.7 | async-start | bytes 2359296 | tf_op jit(solution)/shard_map/reduce_scatter | solution.py:586
  64.1 27.7 %collective-permute-start.15 = (bf16[256,1024]{1,0:T(8,128)(2,1)S(1)}, bf16[256,1024]{1,0:T(8,128)(2,1)S(1)}, u32[]{:S(2)}, u32[]{:S(2)}) collective-permute-start(bf16[256,1024]{1,0:T(8,128)(2,1)S(1)} %pad_maximum_fusion.refs_0_), channel_id=1, source_target_pairs={{0,4},{1,5},{2,6},{3,7},{4,0},{5,1},{6,2},{7,3},{8,12},{9,13},{10,... | collective-permute-start | bytes 1572872 | tf_op jit(solution)/shard_map/ppermute | solution.py:143
  64.1 37.8 %collective-permute-start.14 = (bf16[256,1024]{1,0:T(8,128)(2,1)S(1)}, bf16[256,1024]{1,0:T(8,128)(2,1)S(1)}, u32[]{:S(2)}, u32[]{:S(2)}) collective-permute-start(bf16[256,1024]{1,0:T(8,128)(2,1)S(1)} %pad_maximum_fusion.refs_0_), channel_id=1, source_target_pairs={{0,6},{1,7},{2,0},{3,1},{4,2},{5,3},{6,4},{7,5},{8,14},{9,15},{10,... | collective-permute-start | bytes 1572872 | tf_op jit(solution)/shard_map/ppermute | solution.py:143
  65.6 36.6 %collective-permute-start.13 = (bf16[256,1024]{1,0:T(8,128)(2,1)S(1)}, bf16[256,1024]{1,0:T(8,128)(2,1)S(1)}, u32[]{:S(2)}, u32[]{:S(2)}) collective-permute-start(bf16[256,1024]{1,0:T(8,128)(2,1)S(1)} %pad_maximum_fusion.refs_0_), channel_id=1, source_target_pairs={{0,2},{1,3},{2,4},{3,5},{4,6},{5,7},{6,0},{7,1},{8,10},{9,11},{10,... | collective-permute-start | bytes 1572872 | tf_op jit(solution)/shard_map/ppermute | solution.py:143
  145.4 22.5 %collective-permute-start.26 = (bf16[128,1024]{1,0:T(8,128)(2,1)}, bf16[128,1024]{1,0:T(8,128)(2,1)S(1)}, u32[]{:S(2)}, u32[]{:S(2)}) collective-permute-start(bf16[128,1024]{1,0:T(8,128)(2,1)} %get-tuple-element.195), channel_id=1, source_target_pairs={{0,16},{8,24},{16,32},{24,40},{32,48},{40,56},{48,0},{56,8},{1,17}... | collective-permute-start | bytes 786440 | tf_op jit(solution)/shard_map/ppermute | solution.py:94
  146.5 21.4 %collective-permute-start.25 = (bf16[128,1024]{1,0:T(8,128)(2,1)}, bf16[128,1024]{1,0:T(8,128)(2,1)S(1)}, u32[]{:S(2)}, u32[]{:S(2)}) collective-permute-start(bf16[128,1024]{1,0:T(8,128)(2,1)} %get-tuple-element.196), channel_id=1, source_target_pairs={{0,48},{8,56},{16,0},{24,8},{32,16},{40,24},{48,32},{56,40},{1,49}... | collective-permute-start | bytes 786440 | tf_op jit(solution)/shard_map/ppermute | solution.py:94
  148.1 19.9 %collective-permute-start.24 = (bf16[128,1024]{1,0:T(8,128)(2,1)S(1)}, bf16[128,1024]{1,0:T(8,128)(2,1)S(1)}, u32[]{:S(2)}, u32[]{:S(2)}) collective-permute-start(bf16[128,1024]{1,0:T(8,128)(2,1)S(1)} %get-tuple-element.197), channel_id=1, source_target_pairs={{0,32},{8,40},{16,48},{24,56},{32,0},{40,8},{48,16},{56,24},{1,33}... | collective-permute-start | bytes 786440 | tf_op jit(solution)/shard_map/ppermute | solution.py:94
  158.8 56.6 %all-to-all-start.2 = ((bf16[8,128,1792]{2,1,0:T(8,128)(2,1)}), bf16[8,128,1792]{2,1,0:T(8,128)(2,1)}, u32[]{:S(2)}, u32[]{:S(2)}) async-start(bf16[8,128,1792]{2,1,0:T(8,128)(2,1)} %shard_map.240), calls=%async_computation.4 | async-start | bytes 7340032 | tf_op jit(solution)/shard_map/all_to_all | solution.py:180
  167.9 156.8 %reduce-scatter.5.cloned.1.call-start = ((), (), s32[]{:S(2)}) async-start(), calls=%async_computation.8 | async-start | bytes 2359296 | tf_op jit(solution)/shard_map/reduce_scatter | solution.py:623
  198.0 13.0 %collective-permute-start.34 = (bf16[128,1024]{1,0:T(8,128)(2,1)S(1)}, bf16[128,1024]{1,0:T(8,128)(2,1)S(1)}, u32[]{:S(2)}, u32[]{:S(2)}) collective-permute-start(bf16[128,1024]{1,0:T(8,128)(2,1)S(1)} %copy-done.29), channel_id=1, source_target_pairs={{0,48},{8,56},{16,0},{24,8},{32,16},{40,24},{48,32},{56,40},{1,49}... | collective-permute-start | bytes 786440 | tf_op jit(solution)/shard_map/ppermute | solution.py:94
  199.2 15.2 %collective-permute-start.32 = (bf16[128,1024]{1,0:T(8,128)(2,1)S(1)}, bf16[128,1024]{1,0:T(8,128)(2,1)S(1)}, u32[]{:S(2)}, u32[]{:S(2)}) collective-permute-start(bf16[128,1024]{1,0:T(8,128)(2,1)S(1)} %copy-done.29), channel_id=1, source_target_pairs={{0,16},{8,24},{16,32},{24,40},{32,48},{40,56},{48,0},{56,8},{1,17}... | collective-permute-start | bytes 786440 | tf_op jit(solution)/shard_map/ppermute | solution.py:94
  199.5 19.0 %collective-permute-start.31 = (bf16[128,1024]{1,0:T(8,128)(2,1)S(1)}, bf16[128,1024]{1,0:T(8,128)(2,1)S(1)}, u32[]{:S(2)}, u32[]{:S(2)}) collective-permute-start(bf16[128,1024]{1,0:T(8,128)(2,1)S(1)} %copy-done.29), channel_id=1, source_target_pairs={{0,8},{8,0},{16,24},{24,16},{32,40},{40,32},{48,56},{56,48},{1,9},... | collective-permute-start | bytes 786440 | tf_op jit(solution)/shard_map/ppermute | solution.py:90
  205.3 13.2 %collective-permute-start.37 = (bf16[128,1024]{1,0:T(8,128)(2,1)S(1)}, bf16[128,1024]{1,0:T(8,128)(2,1)S(1)}, u32[]{:S(2)}, u32[]{:S(2)}) collective-permute-start(bf16[128,1024]{1,0:T(8,128)(2,1)S(1)} %collective-permute-done.36.refs_14_), channel_id=1, source_target_pairs={{0,8},{8,0},{16,24},{24,16},{32,40},{40,32},{48,56},{56,48},{1,9},... | collective-permute-start | bytes 786440 | tf_op jit(solution)/shard_map/ppermute | solution.py:90
  218.6 22.7 %collective-permute-start.38 = (bf16[128,1152]{1,0:T(8,128)(2,1)}, bf16[128,1152]{1,0:T(8,128)(2,1)S(1)}, u32[]{:S(2)}, u32[]{:S(2)}) collective-permute-start(bf16[128,1152]{1,0:T(8,128)(2,1)} %get-tuple-element.188.own), channel_id=1, source_target_pairs={{0,64},{64,0},{1,65},{65,1},{2,66},{66,2},{3,67},{67,3},{4,68},{68... | collective-permute-start | bytes 884744 | tf_op jit(solution)/shard_map/ppermute | solution.py:138
  219.1 14.4 %collective-permute-start.40 = (bf16[128,576]{1,0:T(8,128)(2,1)}, bf16[128,576]{1,0:T(8,128)(2,1)S(1)}, u32[]{:S(2)}, u32[]{:S(2)}) collective-permute-start(bf16[128,576]{1,0:T(8,128)(2,1)} %get-tuple-element.179), channel_id=1, source_target_pairs={{0,64},{1,72},{2,80},{3,88},{4,96},{5,104},{6,112},{7,120},{8,65},... | collective-permute-start | bytes 442376 | tf_op jit(solution)/shard_map/ppermute | solution.py:134
  220.9 20.4 %collective-permute-start.39 = (bf16[128,576]{1,0:T(8,128)(2,1)}, bf16[128,576]{1,0:T(8,128)(2,1)S(1)}, u32[]{:S(2)}, u32[]{:S(2)}) collective-permute-start(bf16[128,576]{1,0:T(8,128)(2,1)} %get-tuple-element.179), channel_id=1, source_target_pairs={{0,0},{1,8},{2,16},{3,24},{4,32},{5,40},{6,48},{7,56},{8,1},{9,9},... | collective-permute-start | bytes 442376 | tf_op jit(solution)/shard_map/ppermute | solution.py:134
  241.3 30.8 %all-to-all-start.3 = ((bf16[8,128,512]{2,1,0:T(8,128)(2,1)}), bf16[8,128,512]{2,1,0:T(8,128)(2,1)S(1)}, u32[]{:S(2)}, u32[]{:S(2)}) async-start(bf16[8,128,512]{2,1,0:T(8,128)(2,1)} %shard_map.244), calls=%async_computation.5 | async-start | bytes 2097152 | tf_op jit(solution)/shard_map/all_to_all | solution.py:180
  249.7 14.0 %collective-permute-start.56 = (bf16[128,1728]{1,0:T(8,128)(2,1)}, bf16[128,1728]{1,0:T(8,128)(2,1)S(1)}, u32[]{:S(2)}, u32[]{:S(2)}) collective-permute-start(bf16[128,1728]{1,0:T(8,128)(2,1)} %shard_map.248.refs_1_), channel_id=1, source_target_pairs={{0,32},{8,40},{16,48},{24,56},{32,0},{40,8},{48,16},{56,24},{1,33}... | collective-permute-start | bytes 1327112 | tf_op jit(solution)/shard_map/ppermute | solution.py:94
  249.7 20.9 %collective-permute-start.54 = (bf16[128,1728]{1,0:T(8,128)(2,1)}, bf16[128,1728]{1,0:T(8,128)(2,1)S(1)}, u32[]{:S(2)}, u32[]{:S(2)}) collective-permute-start(bf16[128,1728]{1,0:T(8,128)(2,1)} %shard_map.248.refs_1_), channel_id=1, source_target_pairs={{0,48},{8,56},{16,0},{24,8},{32,16},{40,24},{48,32},{56,40},{1,49}... | collective-permute-start | bytes 1327112 | tf_op jit(solution)/shard_map/ppermute | solution.py:94
  251.0 25.9 %collective-permute-start.52 = (bf16[128,1728]{1,0:T(8,128)(2,1)}, bf16[128,1728]{1,0:T(8,128)(2,1)S(1)}, u32[]{:S(2)}, u32[]{:S(2)}) collective-permute-start(bf16[128,1728]{1,0:T(8,128)(2,1)} %shard_map.248.refs_1_), channel_id=1, source_target_pairs={{0,16},{8,24},{16,32},{24,40},{32,48},{40,56},{48,0},{56,8},{1,17}... | collective-permute-start | bytes 1327112 | tf_op jit(solution)/shard_map/ppermute | solution.py:94
  251.1 46.6 %collective-permute-start.51 = (bf16[128,1728]{1,0:T(8,128)(2,1)}, bf16[128,1728]{1,0:T(8,128)(2,1)}, u32[]{:S(2)}, u32[]{:S(2)}) collective-permute-start(bf16[128,1728]{1,0:T(8,128)(2,1)} %shard_map.248.refs_1_), channel_id=1, source_target_pairs={{0,8},{8,0},{16,24},{24,16},{32,40},{40,32},{48,56},{56,48},{1,9},... | collective-permute-start | bytes 1327112 | tf_op jit(solution)/shard_map/ppermute | solution.py:90
  263.6 38.5 %collective-permute-start.57 = (bf16[128,1728]{1,0:T(8,128)(2,1)S(1)}, bf16[128,1728]{1,0:T(8,128)(2,1)}, u32[]{:S(2)}, u32[]{:S(2)}) collective-permute-start(bf16[128,1728]{1,0:T(8,128)(2,1)S(1)} %collective-permute-done.56.refs_7_), channel_id=1, source_target_pairs={{0,8},{8,0},{16,24},{24,16},{32,40},{40,32},{48,56},{56,48},{1,9},... | collective-permute-start | bytes 1327112 | tf_op jit(solution)/shard_map/ppermute | solution.py:90
  270.6 31.6 %collective-permute-start.55 = (bf16[128,1728]{1,0:T(8,128)(2,1)S(1)}, bf16[128,1728]{1,0:T(8,128)(2,1)}, u32[]{:S(2)}, u32[]{:S(2)}) collective-permute-start(bf16[128,1728]{1,0:T(8,128)(2,1)S(1)} %collective-permute-done.54.refs_5_), channel_id=1, source_target_pairs={{0,8},{8,0},{16,24},{24,16},{32,40},{40,32},{48,56},{56,48},{1,9},... | collective-permute-start | bytes 1327112 | tf_op jit(solution)/shard_map/ppermute | solution.py:90
  276.9 18.6 %collective-permute-start.41 = (bf16[128,384]{1,0:T(8,128)(2,1)}, bf16[128,384]{1,0:T(8,128)(2,1)S(1)}, u32[]{:S(2)}, u32[]{:S(2)}) collective-permute-start(bf16[128,384]{1,0:T(8,128)(2,1)} %get-tuple-element.181.own), channel_id=1, source_target_pairs={{0,64},{64,0},{1,65},{65,1},{2,66},{66,2},{3,67},{67,3},{4,68},{68... | collective-permute-start | bytes 294920 | tf_op jit(solution)/shard_map/ppermute | solution.py:138
  290.3 21.1 %collective-permute-start.53 = (bf16[128,1728]{1,0:T(8,128)(2,1)S(1)}, bf16[128,1728]{1,0:T(8,128)(2,1)}, u32[]{:S(2)}, u32[]{:S(2)}) collective-permute-start(bf16[128,1728]{1,0:T(8,128)(2,1)S(1)} %collective-permute-done.52.refs_3_), channel_id=1, source_target_pairs={{0,8},{8,0},{16,24},{24,16},{32,40},{40,32},{48,56},{56,48},{1,9},... | collective-permute-start | bytes 1327112 | tf_op jit(solution)/shard_map/ppermute | solution.py:90
  302.1 15.9 %collective-permute-start.44 = (bf16[128,512]{1,0:T(8,128)(2,1)}, bf16[128,512]{1,0:T(8,128)(2,1)S(1)}, u32[]{:S(2)}, u32[]{:S(2)}) collective-permute-start(bf16[128,512]{1,0:T(8,128)(2,1)} %shard_map.246.refs_1_), channel_id=1, source_target_pairs={{0,8},{8,0},{16,24},{24,16},{32,40},{40,32},{48,56},{56,48},{1,9},... | collective-permute-start | bytes 393224 | tf_op jit(solution)/shard_map/ppermute | solution.py:90
  303.9 14.2 %collective-permute-start.50 = (bf16[128,512]{1,0:T(8,128)(2,1)S(1)}, bf16[128,512]{1,0:T(8,128)(2,1)S(1)}, u32[]{:S(2)}, u32[]{:S(2)}) collective-permute-start(bf16[128,512]{1,0:T(8,128)(2,1)S(1)} %collective-permute-done.49.refs_7_), channel_id=1, source_target_pairs={{0,8},{8,0},{16,24},{24,16},{32,40},{40,32},{48,56},{56,48},{1,9},... | collective-permute-start | bytes 393224 | tf_op jit(solution)/shard_map/ppermute | solution.py:90
  (103 other events, 1029.2 us)
Sparse Core Ops, SparseCore 0:
  35.0 70.9 all-gather.1
  141.3 38.8 reduce-scatter.2
  196.7 35.7 reduce-scatter.4
